TPU v7x, 32 devices: a whole 2x2x4 slice. The times are simulated.
32 devices in a mesh: member: 8 (over z, x), tile: 4 (over y, core).
Axes of the slice: x: 2, y: 2, z: 4, core: 2. Of those that a mesh axis runs over, the one named last changes fastest.
Arguments:
- saturation: float32 [8, 32, 64, 128], P('member', 'tile'), may hold values from 0.05 to 0.95
- mobility: float32 [8, 32, 64, 128], P('member', 'tile'), may hold values from 0.5 to 4
- pore_scale: float32 [8, 32, 64, 128], P('member', 'tile'), may hold values from 0.5 to 1.5
- flux_x: float32 [8, 32, 64, 128], P('member', 'tile'), may hold values from -0.15 to 0.15
- flux_y: float32 [8, 32, 64, 128], P('member', 'tile'), may hold values from -0.15 to 0.15
- flux_z: float32 [8, 32, 64, 128], P('member', 'tile'), may hold values from -0.15 to 0.15
- conn_cell: int32 [1024], P('tile'), may hold values from 0 to 65535
- conn_well: int32 [1024], P('tile'), may hold values from 0 to 31
- conn_factor: float32 [1024], P('tile'), may hold values from 0.02 to 0.2
- obs_error: float32 [32, 3], P('tile'), may hold values from 0.3 to 3
Outputs:
- new_saturation: float32 [8, 32, 64, 128], P('member', 'tile')
- well_rates: float32 [8, 32, 3], P('member', 'tile')
- gram: float32 [8, 8], P('member')
Inputs may be any that keep to these rules, and one draw needn't show every extreme that they name: `conn_cell`: a cell index within the block of grid rows of the tile that holds the connection, flattened over (row, layer, column). `conn_well`: a well index; any tile may hold connections of any well.
All inputs are finite; a program needn't handle non-finite values.
Results may differ from a plain program's by a relative error of at most 0.0003.
Values sent between devices are 32-bit elements; how exact they have to be, the bound alone decides.
A program may use at most 64 MiB of HBM per device.

v0:
```python
import jax
import jax.numpy as jnp
from jax import lax
from jax.sharding import PartitionSpec as P

SUBSTEPS = 3


def with_halo(cells, sides, width):
    for axis, dim in sides:
        count = lax.axis_size(axis)
        ends = count - 1
        head = lax.slice_in_dim(cells, 0, width, axis=dim)
        tail = lax.slice_in_dim(cells, cells.shape[dim] - width, cells.shape[dim], axis=dim)
        cells = jnp.concatenate(
            [
                lax.ppermute(tail, axis, [(i, (i + 1) % count) for i in range(ends)]),
                cells,
                lax.ppermute(head, axis, [((i + 1) % count, i) for i in range(ends)]),
            ],
            axis=dim,
        )
    return cells


def frac(sat, mob):
    wet = sat * sat
    dry = (1.0 - sat) * (1.0 - sat)
    return wet / (wet + mob * dry)


def lower(field, axis):
    count = field.shape[axis]
    zero = jnp.zeros_like(lax.slice_in_dim(field, 0, 1, axis=axis))
    return jnp.concatenate([zero, lax.slice_in_dim(field, 0, count - 1, axis=axis)], axis=axis)


def upper(field, axis):
    count = field.shape[axis]
    zero = jnp.zeros_like(lax.slice_in_dim(field, 0, 1, axis=axis))
    return jnp.concatenate([lax.slice_in_dim(field, 1, count, axis=axis), zero], axis=axis)


def divergence(flow, flux, axis):
    face = jnp.maximum(flux, 0.0) * lower(flow, axis) + jnp.minimum(flux, 0.0) * flow
    return upper(face, axis) - face


def advance(sat_ext, mob_ext, qx_ext, qy_in, qz_in, pore_in):
    flow_ext = frac(sat_ext, mob_ext)
    crossing = qx_ext[:, 1:]
    face = (
        jnp.maximum(crossing, 0.0) * flow_ext[:, :-1] + jnp.minimum(crossing, 0.0) * flow_ext[:, 1:]
    )
    flow_in = flow_ext[:, 1:-1]
    total = (
        face[:, 1:] - face[:, :-1] + divergence(flow_in, qz_in, 2) + divergence(flow_in, qy_in, 3)
    )
    return sat_ext[:, 1:-1] - pore_in * total


def body(
    saturation,
    mobility,
    pore_scale,
    flux_x,
    flux_y,
    flux_z,
    conn_cell,
    conn_well,
    conn_factor,
    obs_error,
):
    members, rows, layers, columns = saturation.shape
    tiles = lax.axis_size("tile")
    first = lax.axis_index("tile") * rows
    total_rows = rows * tiles

    def place(shape, axis):
        return lax.broadcasted_iota(jnp.int32, shape, axis)

    row_ids = first + place(flux_x.shape, 1)
    qx = jnp.where(row_ids > 0, flux_x, jnp.zeros_like(flux_x))
    qz = jnp.where(place(flux_z.shape, 2) > 0, flux_z, jnp.zeros_like(flux_z))
    qy = jnp.where(place(flux_y.shape, 3) > 0, flux_y, jnp.zeros_like(flux_y))
    states = []
    fixed = with_halo(jnp.stack((qx, mobility)), (("tile", 2),), 1)
    qx_ext = fixed[0]
    mob_ext = fixed[1]
    global_rows = first - 1 + place(mob_ext.shape, 1)
    inside = (global_rows >= 0) & (global_rows < total_rows)
    mob_ext = jnp.where(inside, mob_ext, jnp.ones_like(mob_ext))
    current = saturation
    for step in range(SUBSTEPS):
        sat_ext = with_halo(current, (("tile", 1),), 1)
        current = advance(sat_ext, mob_ext, qx_ext, qy, qz, pore_scale)
        states.append(current)
    new_saturation = states[-1]
    mob_flat = jnp.take(mobility.reshape(members, -1), conn_cell, axis=1)
    parts = []
    for state in states:
        picked = jnp.take(state.reshape(members, -1), conn_cell, axis=1)
        parts.append(conn_factor[None, :] * frac(picked, mob_flat))
    contrib = jnp.stack(parts, -1)
    table = jnp.transpose(contrib, (1, 0, 2)).reshape(conn_cell.shape[0], -1)
    wells_dev = obs_error.shape[0]
    targets = lax.iota(jnp.int32, wells_dev * tiles)
    onehot = (conn_well[None, :] == targets[:, None]).astype(jnp.float32)
    whole = lax.psum(jnp.dot(onehot, table, precision=lax.Precision.HIGHEST), "tile")
    mine = lax.dynamic_slice_in_dim(whole, lax.axis_index("tile") * wells_dev, wells_dev, 0)
    well_rates = jnp.transpose(mine.reshape(wells_dev, members, SUBSTEPS), (1, 0, 2))
    scaled = (well_rates / obs_error[None]).reshape(members, -1)
    ensemble = members * lax.axis_size("member")
    gathered = lax.all_gather(scaled, "member", axis=0, tiled=True)
    centered = gathered - jnp.mean(gathered, axis=0, keepdims=True)
    own = lax.dynamic_slice_in_dim(centered, lax.axis_index("member") * members, members, 0)
    partial_gram = jnp.dot(own, centered.T, precision=lax.Precision.HIGHEST)
    gram = lax.psum(partial_gram, "tile") / (ensemble - 1.0)
    return (new_saturation, well_rates, gram)


def solution(mesh):
    in_specs = (
        P("member", "tile", None, None),
        P("member", "tile", None, None),
        P("member", "tile", None, None),
        P("member", "tile", None, None),
        P("member", "tile", None, None),
        P("member", "tile", None, None),
        P("tile"),
        P("tile"),
        P("tile"),
        P("tile", None),
    )
    out_specs = (P("member", "tile", None, None), P("member", "tile", None), P("member", None))
    return jax.shard_map(body, mesh=mesh, in_specs=in_specs, out_specs=out_specs, check_vma=False)
```

profile of v0, /device:TPU:0, one launch (start us, length us, event | category | flops | bytes accessed | tf_op | source)
XLA Modules:
  0.0 75.0 jit_solution(16583990507642320487)
XLA Ops:
  0.6 0.8 %fusion.35 = (f32[1,1,64,128]{3,2,1,0:T(8,128)S(1)}, f32[1,1,64,128]{3,2,1,0:T(8,128)S(1)}) fusion(f32[1,8,64,128]{3,2,1,0:T(8,128)} %param.12), kind=kLoop, calls=%fused_computation.95 | loop fusion | bytes 131072 | tf_op jit(solution)/shard_map/slice | solution.py:13
  1.4 1.3 %collective-permute-start.3 = (f32[1,1,64,128]{3,2,1,0:T(8,128)S(1)}, f32[1,1,64,128]{3,2,1,0:T(8,128)S(1)}, u32[]{:S(2)}, u32[]{:S(2)}) collective-permute-start(f32[1,1,64,128]{3,2,1,0:T(8,128)S(1)} %get-tuple-element.27), channel_id=1, source_target_pairs={{1,0},{2,1},{3,2},{5,4},{6,5},{7,6},{9,8},{10,9},{11,10},{13,12},{... | collective-permute-start | bytes 98312 | tf_op jit(solution)/shard_map/ppermute | solution.py:19
  2.7 3.0 %collective-permute-start.2 = (f32[1,1,64,128]{3,2,1,0:T(8,128)S(1)}, f32[1,1,64,128]{3,2,1,0:T(8,128)S(1)}, u32[]{:S(2)}, u32[]{:S(2)}) collective-permute-start(f32[1,1,64,128]{3,2,1,0:T(8,128)S(1)} %get-tuple-element.28), channel_id=1, source_target_pairs={{0,1},{1,2},{2,3},{4,5},{5,6},{6,7},{8,9},{9,10},{10,11},{12,13},{... | collective-permute-start | bytes 98312 | tf_op jit(solution)/shard_map/ppermute | solution.py:17
  5.8 0.0 copy-start
  5.8 1.1 %select_bitcast_fusion = f32[1,1,8,64,128]{4,3,2,1,0:T(8,128)S(1)} fusion(f32[1,8,64,128]{3,2,1,0:T(8,128)} %param.15, pred[8]{0:T(512)(128)(4,1)S(1)} %add_compare_fusion), kind=kLoop, calls=%fused_computation.45 | loop fusion | flops 65536 | bytes 524296 | tf_op jit(solution)/shard_map/stack | solution.py:87
  6.9 0.0 copy-start.5
  6.9 4.6 %collective-permute-start = (f32[2,1,1,64,128]{4,3,2,1,0:T(8,128)S(1)}, f32[2,1,1,64,128]{4,3,2,1,0:T(8,128)S(1)}, u32[]{:S(2)}, u32[]{:S(2)}) collective-permute-start(f32[2,1,1,64,128]{4,3,2,1,0:T(8,128)S(1)} %get-tuple-element.15), channel_id=1, source_target_pairs={{0,1},{1,2},{2,3},{4,5},{5,6},{6,7},{8,9},{9,10},{10,11},{12,13},{... | collective-permute-start | bytes 196616 | tf_op jit(solution)/shard_map/ppermute | solution.py:17
  11.5 1.3 %collective-permute-start.1 = (f32[2,1,1,64,128]{4,3,2,1,0:T(8,128)S(1)}, f32[2,1,1,64,128]{4,3,2,1,0:T(8,128)S(1)}, u32[]{:S(2)}, u32[]{:S(2)}) collective-permute-start(f32[2,1,1,64,128]{4,3,2,1,0:T(8,128)S(1)} %get-tuple-element.16), channel_id=1, source_target_pairs={{1,0},{2,1},{3,2},{5,4},{6,5},{7,6},{9,8},{10,9},{11,10},{13,12},{... | collective-permute-start | bytes 196616 | tf_op jit(solution)/shard_map/ppermute | solution.py:19
  12.9 0.0 copy-start.6
  12.9 0.7 copy-done.6
  13.5 0.0 collective-permute-done.2
  13.6 0.0 collective-permute-done.3
  13.6 0.0 collective-permute-done
  13.6 1.0 %collective-permute-done.1 = f32[2,1,1,64,128]{4,3,2,1,0:T(8,128)S(1)} collective-permute-done((f32[2,1,1,64,128]{4,3,2,1,0:T(8,128)S(1)}, f32[2,1,1,64,128]{4,3,2,1,0:T(8,128)S(1)}, u32[]{:S(2)}, u32[]{:S(2)}) %collective-permute-start.1) | collective-permute-done | bytes 65568 | tf_op jit(solution)/shard_map/ppermute | solution.py:19
  14.7 0.1 pad_maximum_fusion
  14.7 0.1 add_divide_fusion.2
  14.9 0.0 copy-start.2
  14.9 0.0 copy-start.3
  15.0 0.9 %copy-done.2 = f32[1,8,64,128]{3,2,1,0:T(8,128)S(1)} copy-done((f32[1,8,64,128]{3,2,1,0:T(8,128)S(1)}, f32[1,8,64,128]{3,2,1,0:T(8,128)}, u32[]{:S(2)}) %copy-start.2) | copy-done | bytes 262168
  15.9 0.1 copy-done.3
  16.0 0.2 multiply_add_fusion.5
  16.2 0.1 slice.179
  16.3 0.0 copy-start.4
  16.3 0.1 fusion.3
  16.4 0.9 %copy-done.4 = f32[1,8,64,128]{3,2,1,0:T(8,128)S(1)} copy-done((f32[1,8,64,128]{3,2,1,0:T(8,128)S(1)}, f32[1,8,64,128]{3,2,1,0:T(8,128)}, u32[]{:S(2)}) %copy-start.4) | copy-done | bytes 262168
  17.3 0.1 fusion.15
  17.4 4.8 %collective-permute-start.4 = (f32[1,1,64,128]{3,2,1,0:T(8,128)S(1)}, f32[1,1,64,128]{3,2,1,0:T(8,128)S(1)}, u32[]{:S(2)}, u32[]{:S(2)}) collective-permute-start(f32[1,1,64,128]{3,2,1,0:T(8,128)S(1)} %get-tuple-element.25), channel_id=1, source_target_pairs={{0,1},{1,2},{2,3},{4,5},{5,6},{6,7},{8,9},{9,10},{10,11},{12,13},{... | collective-permute-start | bytes 98312 | tf_op jit(solution)/shard_map/ppermute | solution.py:17
  22.3 1.3 %collective-permute-start.5 = (f32[1,1,64,128]{3,2,1,0:T(8,128)S(1)}, f32[1,1,64,128]{3,2,1,0:T(8,128)S(1)}, u32[]{:S(2)}, u32[]{:S(2)}) collective-permute-start(f32[1,1,64,128]{3,2,1,0:T(8,128)S(1)} %get-tuple-element.26), channel_id=1, source_target_pairs={{1,0},{2,1},{3,2},{5,4},{6,5},{7,6},{9,8},{10,9},{11,10},{13,12},{... | collective-permute-start | bytes 98312 | tf_op jit(solution)/shard_map/ppermute | solution.py:19
  23.6 1.7 %gather_fusion.1 = f32[256]{0:T(256)S(1)} fusion(f32[65536]{0:T(1024)S(1)} %bitcast.54, s32[1024]{0:T(1024)S(1)} %pad_clamp_fusion), kind=kCustom, calls=%fused_computation.1.clone | custom fusion | bytes 3072 | tf_op jit(solution)/shard_map/jit(_take)/gather | solution.py:99
  25.3 1.7 %gather_fusion = f32[256]{0:T(256)S(1)} fusion(f32[65536]{0:T(1024)S(1)} %bitcast.50, s32[1024]{0:T(1024)S(1)} %pad_clamp_fusion), kind=kCustom, calls=%fused_computation.clone | custom fusion | bytes 3072 | tf_op jit(solution)/shard_map/jit(_take)/gather | solution.py:102
  27.1 0.0 collective-permute-done.4
  27.1 0.0 collective-permute-done.5
  27.1 0.1 add_divide_fusion.1
  27.3 0.1 fusion.2
  27.3 0.2 multiply_add_fusion.3
  27.5 0.1 slice.190
  27.7 0.1 fusion.11
  27.8 3.0 %collective-permute-start.6 = (f32[1,1,64,128]{3,2,1,0:T(8,128)S(1)}, f32[1,1,64,128]{3,2,1,0:T(8,128)S(1)}, u32[]{:S(2)}, u32[]{:S(2)}) collective-permute-start(f32[1,1,64,128]{3,2,1,0:T(8,128)S(1)} %get-tuple-element.23), channel_id=1, source_target_pairs={{0,1},{1,2},{2,3},{4,5},{5,6},{6,7},{8,9},{9,10},{10,11},{12,13},{... | collective-permute-start | bytes 98312 | tf_op jit(solution)/shard_map/ppermute | solution.py:17
  30.9 1.3 %collective-permute-start.7 = (f32[1,1,64,128]{3,2,1,0:T(8,128)S(1)}, f32[1,1,64,128]{3,2,1,0:T(8,128)S(1)}, u32[]{:S(2)}, u32[]{:S(2)}) collective-permute-start(f32[1,1,64,128]{3,2,1,0:T(8,128)S(1)} %get-tuple-element.24), channel_id=1, source_target_pairs={{1,0},{2,1},{3,2},{5,4},{6,5},{7,6},{9,8},{10,9},{11,10},{13,12},{... | collective-permute-start | bytes 98312 | tf_op jit(solution)/shard_map/ppermute | solution.py:19
  32.2 1.7 %gather_fusion.2 = f32[256]{0:T(256)S(1)} fusion(f32[65536]{0:T(1024)S(1)} %bitcast.51, s32[1024]{0:T(1024)S(1)} %pad_clamp_fusion), kind=kCustom, calls=%fused_computation.2.clone | custom fusion | bytes 3072 | tf_op jit(solution)/shard_map/jit(_take)/gather | solution.py:102
  33.9 0.0 collective-permute-done.6
  33.9 0.8 %collective-permute-done.7 = f32[1,1,64,128]{3,2,1,0:T(8,128)S(1)} collective-permute-done((f32[1,1,64,128]{3,2,1,0:T(8,128)S(1)}, f32[1,1,64,128]{3,2,1,0:T(8,128)S(1)}, u32[]{:S(2)}, u32[]{:S(2)}) %collective-permute-start.7) | collective-permute-done | bytes 32800 | tf_op jit(solution)/shard_map/ppermute | solution.py:19
  34.7 0.1 add_divide_fusion
  34.9 0.1 fusion.1
  35.0 0.2 multiply_add_fusion.1
  35.2 0.1 slice.201
  35.3 0.1 fusion.7
  35.5 0.0 copy-start.1
  35.5 1.7 %gather_fusion.3 = f32[256]{0:T(256)S(1)} fusion(f32[65536]{0:T(1024)S(1)} %bitcast.55, s32[1024]{0:T(1024)S(1)} %pad_clamp_fusion), kind=kCustom, calls=%fused_computation.3.clone | custom fusion | bytes 3072 | tf_op jit(solution)/shard_map/jit(_take)/gather | solution.py:102
  37.2 0.0 copy-done.1
  37.3 0.0 copy-start.8
  37.3 0.7 copy-done.8
  38.0 0.0 copy-start.9
  38.0 0.7 copy-done.9
  38.6 0.1 fusion.16
  38.8 8.4 %psum.14 = f32[32,3]{0,1:T(4,128)S(1)} all-reduce(f32[32,3]{0,1:T(4,128)S(1)} %fusion.16), channel_id=1, replica_groups=mesh['member'=8,'tile'=4] {'tile'}, use_global_device_ids=true, to_apply=%region_0.2 | all-reduce | flops 96 | bytes 768 | tf_op jit(solution)/shard_map/psum | solution.py:109
  47.2 0.1 dynamic-slice_divide_fusion
  47.2 0.1 copy.17
  47.3 0.1 reshape.408
  47.4 20.7 %all-gather = f32[8,1,24]{2,1,0:T(1,128)S(1)} all-gather(f32[1,1,24]{2,1,0:T(1,128)S(1)} %reshape.408), channel_id=1, replica_groups=mesh['member'=8,'tile'=4] {'member'}, dimensions={0}, use_global_device_ids=true | all-gather | bytes 864 | tf_op jit(solution)/shard_map/all_gather | solution.py:114
  68.1 0.1 fusion.28
  68.3 0.6 copy.18
  68.8 5.6 %psum.15 = f32[1,8]{1,0:T(1,128)S(1)} all-reduce(f32[1,8]{1,0:T(1,128)S(1)} %fusion.28), channel_id=1, replica_groups=mesh['member'=8,'tile'=4] {'tile'}, use_global_device_ids=true, to_apply=%region_2.4 | all-reduce | flops 8 | bytes 64 | tf_op jit(solution)/shard_map/psum | solution.py:118
  74.5 0.5 broadcast_multiply_fusion
  (32 shorter events, 0.4 us)
Async XLA Ops:
  1.4 12.2 %collective-permute-start.3 = (f32[1,1,64,128]{3,2,1,0:T(8,128)S(1)}, f32[1,1,64,128]{3,2,1,0:T(8,128)S(1)}, u32[]{:S(2)}, u32[]{:S(2)}) collective-permute-start(f32[1,1,64,128]{3,2,1,0:T(8,128)S(1)} %get-tuple-element.27), channel_id=1, source_target_pairs={{1,0},{2,1},{3,2},{5,4},{6,5},{7,6},{9,8},{10,9},{11,10},{13,12},{... | collective-permute-start | bytes 98312 | tf_op jit(solution)/shard_map/ppermute | solution.py:19
  2.7 10.9 %collective-permute-start.2 = (f32[1,1,64,128]{3,2,1,0:T(8,128)S(1)}, f32[1,1,64,128]{3,2,1,0:T(8,128)S(1)}, u32[]{:S(2)}, u32[]{:S(2)}) collective-permute-start(f32[1,1,64,128]{3,2,1,0:T(8,128)S(1)} %get-tuple-element.28), channel_id=1, source_target_pairs={{0,1},{1,2},{2,3},{4,5},{5,6},{6,7},{8,9},{9,10},{10,11},{12,13},{... | collective-permute-start | bytes 98312 | tf_op jit(solution)/shard_map/ppermute | solution.py:17
  5.8 1.1 %copy-start = (f32[1,8,64,128]{3,2,1,0:T(8,128)S(1)}, f32[1,8,64,128]{3,2,1,0:T(8,128)}, u32[]{:S(2)}) copy-start(f32[1,8,64,128]{3,2,1,0:T(8,128)} %param.13) | copy-start | bytes 786436
  6.9 6.7 %copy-start.5 = (f32[1,8,64,128]{3,2,1,0:T(8,128)S(1)}, f32[1,8,64,128]{3,2,1,0:T(8,128)}, u32[]{:S(2)}) copy-start(f32[1,8,64,128]{3,2,1,0:T(8,128)} %param.12) | copy-start | bytes 786436
  6.9 6.7 %collective-permute-start = (f32[2,1,1,64,128]{4,3,2,1,0:T(8,128)S(1)}, f32[2,1,1,64,128]{4,3,2,1,0:T(8,128)S(1)}, u32[]{:S(2)}, u32[]{:S(2)}) collective-permute-start(f32[2,1,1,64,128]{4,3,2,1,0:T(8,128)S(1)} %get-tuple-element.15), channel_id=1, source_target_pairs={{0,1},{1,2},{2,3},{4,5},{5,6},{6,7},{8,9},{9,10},{10,11},{12,13},{... | collective-permute-start | bytes 196616 | tf_op jit(solution)/shard_map/ppermute | solution.py:17
  11.5 3.1 %collective-permute-start.1 = (f32[2,1,1,64,128]{4,3,2,1,0:T(8,128)S(1)}, f32[2,1,1,64,128]{4,3,2,1,0:T(8,128)S(1)}, u32[]{:S(2)}, u32[]{:S(2)}) collective-permute-start(f32[2,1,1,64,128]{4,3,2,1,0:T(8,128)S(1)} %get-tuple-element.16), channel_id=1, source_target_pairs={{1,0},{2,1},{3,2},{5,4},{6,5},{7,6},{9,8},{10,9},{11,10},{13,12},{... | collective-permute-start | bytes 196616 | tf_op jit(solution)/shard_map/ppermute | solution.py:19
  12.9 0.7 copy-start.6
  14.9 1.0 %copy-start.2 = (f32[1,8,64,128]{3,2,1,0:T(8,128)S(1)}, f32[1,8,64,128]{3,2,1,0:T(8,128)}, u32[]{:S(2)}) copy-start(f32[1,8,64,128]{3,2,1,0:T(8,128)} %param.17) | copy-start | bytes 786436
  14.9 1.0 %copy-start.3 = (f32[1,8,64,128]{3,2,1,0:T(8,128)S(1)}, f32[1,8,64,128]{3,2,1,0:T(8,128)}, u32[]{:S(2)}) copy-start(f32[1,8,64,128]{3,2,1,0:T(8,128)} %param.16) | copy-start | bytes 786436
  16.3 1.0 %copy-start.4 = (f32[1,8,64,128]{3,2,1,0:T(8,128)S(1)}, f32[1,8,64,128]{3,2,1,0:T(8,128)}, u32[]{:S(2)}) copy-start(f32[1,8,64,128]{3,2,1,0:T(8,128)} %param.14) | copy-start | bytes 786436
  17.4 9.6 %collective-permute-start.4 = (f32[1,1,64,128]{3,2,1,0:T(8,128)S(1)}, f32[1,1,64,128]{3,2,1,0:T(8,128)S(1)}, u32[]{:S(2)}, u32[]{:S(2)}) collective-permute-start(f32[1,1,64,128]{3,2,1,0:T(8,128)S(1)} %get-tuple-element.25), channel_id=1, source_target_pairs={{0,1},{1,2},{2,3},{4,5},{5,6},{6,7},{8,9},{9,10},{10,11},{12,13},{... | collective-permute-start | bytes 98312 | tf_op jit(solution)/shard_map/ppermute | solution.py:17
  22.3 4.8 %collective-permute-start.5 = (f32[1,1,64,128]{3,2,1,0:T(8,128)S(1)}, f32[1,1,64,128]{3,2,1,0:T(8,128)S(1)}, u32[]{:S(2)}, u32[]{:S(2)}) collective-permute-start(f32[1,1,64,128]{3,2,1,0:T(8,128)S(1)} %get-tuple-element.26), channel_id=1, source_target_pairs={{1,0},{2,1},{3,2},{5,4},{6,5},{7,6},{9,8},{10,9},{11,10},{13,12},{... | collective-permute-start | bytes 98312 | tf_op jit(solution)/shard_map/ppermute | solution.py:19
  27.8 6.1 %collective-permute-start.6 = (f32[1,1,64,128]{3,2,1,0:T(8,128)S(1)}, f32[1,1,64,128]{3,2,1,0:T(8,128)S(1)}, u32[]{:S(2)}, u32[]{:S(2)}) collective-permute-start(f32[1,1,64,128]{3,2,1,0:T(8,128)S(1)} %get-tuple-element.23), channel_id=1, source_target_pairs={{0,1},{1,2},{2,3},{4,5},{5,6},{6,7},{8,9},{9,10},{10,11},{12,13},{... | collective-permute-start | bytes 98312 | tf_op jit(solution)/shard_map/ppermute | solution.py:17
  30.9 3.9 %collective-permute-start.7 = (f32[1,1,64,128]{3,2,1,0:T(8,128)S(1)}, f32[1,1,64,128]{3,2,1,0:T(8,128)S(1)}, u32[]{:S(2)}, u32[]{:S(2)}) collective-permute-start(f32[1,1,64,128]{3,2,1,0:T(8,128)S(1)} %get-tuple-element.24), channel_id=1, source_target_pairs={{1,0},{2,1},{3,2},{5,4},{6,5},{7,6},{9,8},{10,9},{11,10},{13,12},{... | collective-permute-start | bytes 98312 | tf_op jit(solution)/shard_map/ppermute | solution.py:19
  35.5 1.7 %copy-start.1 = (f32[1,8,64,128]{3,2,1,0:T(8,128)}, f32[1,8,64,128]{3,2,1,0:T(8,128)S(1)}, u32[]{:S(2)}) copy-start(f32[1,8,64,128]{3,2,1,0:T(8,128)S(1)} %fusion.7) | copy-start | bytes 786436
  37.3 0.7 copy-start.8
  38.0 0.7 copy-start.9
  38.8 8.4 %copy-start.7 = (f32[8,3]{0,1:T(4,128)S(1)}, f32[8,3]{0,1:T(4,128)}, u32[]{:S(2)}) copy-start(f32[8,3]{0,1:T(4,128)} %param.21) | copy-start | bytes 292
where the time goes:
time: 75.5 us; the launch traced here: 75 us
  blocking collectives  34.7 us (46%)
  starting transfers between devices  20.7 us (27%)
  local copies, waits for them, and re-layouts  12.9 us (17%)
  other arithmetic  3.37 us (4%)
  waiting for transfers between devices  1.85 us (2%)
  between operations  1.17 us (2%)
    all_gather x1, blocking collectives, body(): gathered = lax.all_gather(scaled, 'member', axis=0, tiled=True)  20.7 us
    ppermute x4, starting transfers between devices, with_halo(): lax.ppermute(tail, axis, [(i, (i + 1) % count) for i in range(ends)])  15.5 us
    psum x1, blocking collectives, body(): lax.psum(jnp.dot(onehot, table, precision=lax.Precision.HIGHEST), 'tile')  8.4 us
    psum x1, blocking collectives, body(): gram = lax.psum(partial_gram, 'tile') / (ensemble - 1.0)  5.63 us
    gather x3, local copies, waits for them, and re-layouts, body(): picked = jnp.take(state.reshape(members, -1), conn_cell, axis=1)  5.17 us
    ppermute x4, starting transfers between devices, with_halo(): lax.ppermute(head, axis, [((i + 1) % count, i) for i in range(ends)])  5.16 us
    unnamed x24, local copies, waits for them, and re-layouts  4.6 us
    ppermute x4, waiting for transfers between devices, with_halo(): lax.ppermute(head, axis, [((i + 1) % count, i) for i in range(ends)])  1.84 us
  transfers between devices with their start and end apart: 8, of which 2 were waited for; matrix products, arithmetic and copies ran while one was open for 8% of the time, Pallas kernels for 0%

commit v1 on v0

v1 whole, which is shorter than its diff:
```python
import functools

import jax
import jax.numpy as jnp
from jax import lax
from jax.experimental import pallas as pl
from jax.experimental.pallas import tpu as pltpu
from jax.sharding import PartitionSpec as P

SUBSTEPS = 3
LANES = 128
SUBLANES = 8
MESH = pl.DeviceIdType.MESH


def frac(sat, mob):
    wet = sat * sat
    rest = 1.0 - sat
    return wet / (wet + mob * (rest * rest))


def face(flux, below, here):
    return jnp.maximum(flux, 0.0) * below + jnp.minimum(flux, 0.0) * here


def columns_of(row):
    return jnp.transpose(jnp.broadcast_to(row, (LANES, row.shape[1])))


def kernel(
    tiles,
    members,
    sat_hbm,
    mob_hbm,
    pore_hbm,
    qx_hbm,
    qy_hbm,
    qz_hbm,
    cell_hbm,
    well_hbm,
    factor_hbm,
    obs_hbm,
    new_ref,
    rates_ref,
    gram_ref,
    sat,
    mob,
    pore,
    qx,
    qy,
    qz,
    cell_ref,
    well_ref,
    factor_ref,
    obs_ref,
    flow,
    halo_lo,
    halo_hi,
    q_above,
    split,
    pick,
    lane_mask,
    well_mask,
    obs_all,
    sums,
    data,
    in_sem,
    halo_send,
    halo_recv,
    q_send,
    q_recv,
    obs_send,
    obs_recv,
    sum_send,
    sum_recv,
    data_send,
    data_recv,
):
    tile = lax.axis_index("tile")
    member = lax.axis_index("member")
    rows, layers, columns = sat.shape
    last = rows - 1
    wells_dev = obs_ref.shape[1]
    conns = cell_ref.shape[1]
    has_lo = tile > 0
    has_hi = tile < tiles - 1

    loads = [
        pltpu.make_async_copy(src, dst, in_sem.at[n])
        for n, (src, dst) in enumerate(
            (
                (sat_hbm.at[0], sat),
                (mob_hbm.at[0], mob),
                (qx_hbm.at[0], qx),
                (qz_hbm.at[0], qz),
                (qy_hbm.at[0], qy),
                (pore_hbm.at[0], pore),
                (obs_hbm, obs_ref),
                (cell_hbm, cell_ref),
                (well_hbm, well_ref),
                (factor_hbm, factor_ref),
            )
        )
    ]
    for load in loads:
        load.start()

    barrier = pltpu.get_barrier_semaphore()
    for d in range(1, tiles):
        pl.semaphore_signal(
            barrier, inc=1, device_id={"tile": lax.rem(tile + d, tiles)}, device_id_type=MESH
        )
    for d in range(1, members):
        pl.semaphore_signal(
            barrier, inc=1, device_id={"member": lax.rem(member + d, members)}, device_id_type=MESH
        )

    pl.semaphore_wait(barrier, tiles + members - 2)

    def exchange(src, dst_at, peers, axis, me, send_sem, recv_sem):
        copies = []
        for d in range(1, peers):
            copies.append(
                pltpu.make_async_remote_copy(
                    src_ref=src,
                    dst_ref=dst_at,
                    send_sem=send_sem.at[d - 1],
                    recv_sem=recv_sem.at[d - 1],
                    device_id={axis: lax.rem(me + d, peers)},
                    device_id_type=MESH,
                )
            )
            copies[-1].start()
        return copies

    q_copy = pltpu.make_async_remote_copy(
        src_ref=qx_hbm.at[0, 0],
        dst_ref=q_above,
        send_sem=q_send,
        recv_sem=q_recv,
        device_id={"tile": jnp.maximum(tile - 1, 0)},
        device_id_type=MESH,
    )

    def halo_copies(k):
        down = pltpu.make_async_remote_copy(
            src_ref=flow.at[k, 0],
            dst_ref=halo_hi.at[k],
            send_sem=halo_send.at[k, 0],
            recv_sem=halo_recv.at[k, 0],
            device_id={"tile": jnp.maximum(tile - 1, 0)},
            device_id_type=MESH,
        )
        up = pltpu.make_async_remote_copy(
            src_ref=flow.at[k, last],
            dst_ref=halo_lo.at[k],
            send_sem=halo_send.at[k, 1],
            recv_sem=halo_recv.at[k, 1],
            device_id={"tile": jnp.minimum(tile + 1, tiles - 1)},
            device_id_type=MESH,
        )
        return down, up

    halos = [halo_copies(k) for k in range(SUBSTEPS)]

    def send_halo(k):
        down, up = halos[k]

        @pl.when(has_lo)
        def _():
            down.start()

        @pl.when(has_hi)
        def _():
            up.start()

    def set_flow(k, i, value):
        flow[k, i] = value

    def set_split(i, value):
        high = value.astype(jnp.bfloat16)
        at = pl.ds(pl.multiple_of(i * layers, layers), layers)
        split[at, 0:columns] = high
        split[at, columns : 2 * columns] = (value - high.astype(jnp.float32)).astype(jnp.bfloat16)

    loads[0].wait()
    loads[1].wait()
    set_flow(0, 0, frac(sat[0], mob[0]))
    set_flow(0, last, frac(sat[last], mob[last]))
    send_halo(0)

    @pl.when(has_lo)
    def _():
        q_copy.start()

    loads[6].wait()
    obs_all[tile] = jnp.ones((SUBLANES, LANES), jnp.float32)
    obs_all[tile, 0:SUBSTEPS, 0:wells_dev] = obs_ref[...]
    obs_copies = exchange(obs_all.at[tile], obs_all.at[tile], tiles, "tile", tile, obs_send, obs_recv)

    def first_flow(i, carry):
        set_flow(0, i, frac(sat[i], mob[i]))
        return carry

    lax.fori_loop(1, last, first_flow, 0, unroll=True)
    for load in loads[2:6]:
        load.wait()

    col_ids = lax.broadcasted_iota(jnp.int32, (layers, columns), 1)
    lay_ids = lax.broadcasted_iota(jnp.int32, (layers, columns), 0)

    def update(k, i, face_lo, face_hi):
        here = flow[k, i]
        qz_i = jnp.where(lay_ids > 0, qz[i], 0.0)
        qy_i = jnp.where(col_ids > 0, qy[i], 0.0)
        face_z = face(qz_i, pltpu.roll(here, 1, 0), here)
        face_y = face(qy_i, pltpu.roll(here, 1, 1), here)
        total = face_hi - face_lo
        total = total + (pltpu.roll(face_z, layers - 1, 0) - face_z)
        total = total + (pltpu.roll(face_y, columns - 1, 1) - face_y)
        after = sat[i] - pore[i] * total
        if k + 1 < SUBSTEPS:
            sat[i] = after
        else:
            new_ref[0, i] = after
        value = frac(after, mob[i])
        set_flow(k + 1, i, value)
        set_split(i, value)

    def set_masks():
        for load in loads[7:]:
            load.wait()
        lane_ids = lax.broadcasted_iota(jnp.int32, (conns, LANES), 1)
        cell_col = columns_of(cell_ref[...])
        row_col = lax.shift_right_logical(cell_col, columns.bit_length() - 1)
        for b in range(rows * layers // LANES):
            pick[:, b * LANES : (b + 1) * LANES] = jnp.where(
                row_col == lane_ids + b * LANES, 1.0, 0.0
            ).astype(jnp.bfloat16)
        lane_mask[...] = jnp.where(
            cell_col - row_col * columns == lane_ids, columns_of(factor_ref[...]), 0.0
        )
        well_mask[...] = jnp.where(columns_of(well_ref[...]) == lane_ids, 1.0, 0.0)

    step_rates = []
    for k in range(SUBSTEPS):
        def inner(i, face_lo, k=k):
            face_hi = face(qx[i + 1], flow[k, i], flow[k, i + 1])
            update(k, i, face_lo, face_hi)
            return face_hi

        face_one = face(qx[1], flow[k, 0], flow[k, 1])
        face_last = lax.fori_loop(1, last, inner, face_one, unroll=True)
        if k == 0:
            set_masks()

        down, up = halos[k]

        @pl.when(has_lo)
        def _():
            up.wait_recv()

        @pl.when(has_hi)
        def _():
            down.wait_recv()

        if k == 0:

            @pl.when(has_hi)
            def _():
                q_copy.wait_recv()

            @pl.when(jnp.logical_not(has_hi))
            def _():
                q_above[...] = jnp.zeros_like(q_above)

        below = jnp.where(has_lo, halo_lo[k], 0.0)
        above = jnp.where(has_hi, halo_hi[k], 0.0)
        qx_first = jnp.where(has_lo, qx[0], 0.0)
        update(k, 0, face(qx_first, below, flow[k, 0]), face_one)
        update(k, last, face_last, face(q_above[...], flow[k, last], above))
        if k + 1 < SUBSTEPS:
            send_halo(k + 1)
        found = jnp.dot(pick[...], split[...], preferred_element_type=jnp.float32)
        found = (found[:, 0:columns] + found[:, columns : 2 * columns]) * lane_mask[...]
        rate = jnp.sum(found, axis=1, keepdims=True) * well_mask[...]
        step_rates.append(jnp.sum(rate, axis=0, keepdims=True))

    step_rates.append(jnp.zeros((SUBLANES - SUBSTEPS, LANES), jnp.float32))
    sums[tile] = jnp.concatenate(step_rates, axis=0)
    sum_copies = exchange(sums.at[tile], sums.at[tile], tiles, "tile", tile, sum_send, sum_recv)
    for copy in obs_copies:
        copy.wait_recv()
    lane_row = lax.broadcasted_iota(jnp.int32, (SUBLANES, LANES), 1)
    obs_whole = obs_all[0]
    for t in range(1, tiles):
        moved = pltpu.roll(obs_all[t], t * wells_dev, 1)
        obs_whole = jnp.where(lane_row >= t * wells_dev, moved, obs_whole)
    for copy in sum_copies:
        copy.wait_recv()
    whole = sums[0]
    for t in range(1, tiles):
        whole = whole + sums[t]
    data[member] = whole / obs_whole
    data_copies = exchange(
        data.at[member], data.at[member], members, "member", member, data_send, data_recv
    )
    mine = pltpu.roll(whole, lax.rem(LANES - tile * wells_dev, LANES), 1)
    for k in range(SUBSTEPS):
        rates_ref[k] = mine[k : k + 1, 0:wells_dev]

    for copy in data_copies:
        copy.wait_recv()
    mean = data[0]
    for m in range(1, members):
        mean = mean + data[m]
    mean = mean * (1.0 / members)
    own = data[member] - mean
    terms = jnp.concatenate(
        [jnp.sum(own * (data[m] - mean), axis=0, keepdims=True) for m in range(members)], axis=0
    )
    terms = jnp.sum(terms, axis=1, keepdims=True)
    square = (members, LANES)
    diagonal = lax.broadcasted_iota(jnp.int32, square, 0) == lax.broadcasted_iota(
        jnp.int32, square, 1
    )
    line = jnp.sum(jnp.where(diagonal, terms, 0.0), axis=0, keepdims=True)
    gram_ref[...] = line[:, 0:members] / (members - 1.0)

    for down, up in halos:

        @pl.when(has_lo)
        def _():
            down.wait_send()

        @pl.when(has_hi)
        def _():
            up.wait_send()

    @pl.when(has_lo)
    def _():
        q_copy.wait_send()

    for copy in obs_copies + sum_copies + data_copies:
        copy.wait_send()


def body(tiles, members, sat, mob, pore, qx, qy, qz, cell, well, factor, obs):
    block = sat.shape[1:]
    rows, layers, columns = block
    conns = cell.shape[0]
    wells_dev = obs.shape[0]
    f32 = jnp.float32
    dma = pltpu.SemaphoreType.DMA
    hbm_spec = pl.BlockSpec(memory_space=pltpu.HBM)
    vmem_spec = pl.BlockSpec(memory_space=pltpu.VMEM)
    new, rates, gram = pl.pallas_call(
        functools.partial(kernel, tiles, members),
        out_shape=(
            jax.ShapeDtypeStruct(sat.shape, f32),
            jax.ShapeDtypeStruct((SUBSTEPS, 1, wells_dev), f32),
            jax.ShapeDtypeStruct((1, members), f32),
        ),
        in_specs=[hbm_spec] * 10,
        out_specs=(vmem_spec,) * 3,
        scratch_shapes=[pltpu.VMEM(block, f32)] * 6
        + [
            pltpu.VMEM((1, conns), jnp.int32),
            pltpu.VMEM((1, conns), jnp.int32),
            pltpu.VMEM((1, conns), f32),
            pltpu.VMEM((SUBSTEPS, wells_dev), f32),
            pltpu.VMEM((SUBSTEPS + 1,) + block, f32),
            pltpu.VMEM((SUBSTEPS, layers, columns), f32),
            pltpu.VMEM((SUBSTEPS, layers, columns), f32),
            pltpu.VMEM((layers, columns), f32),
            pltpu.VMEM((rows * layers, 2 * columns), jnp.bfloat16),
            pltpu.VMEM((conns, rows * layers), jnp.bfloat16),
            pltpu.VMEM((conns, LANES), f32),
            pltpu.VMEM((conns, LANES), f32),
            pltpu.VMEM((tiles, SUBLANES, LANES), f32),
            pltpu.VMEM((tiles, SUBLANES, LANES), f32),
            pltpu.VMEM((members, SUBLANES, LANES), f32),
            dma((10,)),
            dma((SUBSTEPS, 2)),
            dma((SUBSTEPS, 2)),
            dma(()),
            dma(()),
            dma((tiles - 1,)),
            dma((tiles - 1,)),
            dma((tiles - 1,)),
            dma((tiles - 1,)),
            dma((members - 1,)),
            dma((members - 1,)),
        ],
        compiler_params=pltpu.CompilerParams(
            collective_id=0, has_side_effects=True, vmem_limit_bytes=60 * 1024 * 1024
        ),
        cost_estimate=pl.CostEstimate(
            flops=100 * SUBSTEPS * rows * layers * columns,
            bytes_accessed=28 * rows * layers * columns,
            transcendentals=0,
        ),
        name="transport",
    )(sat, mob, pore, qx, qy, qz, cell.reshape(1, -1), well.reshape(1, -1), factor.reshape(1, -1), obs.T)
    return new, jnp.transpose(rates, (1, 2, 0)), gram


def solution(mesh):
    field = P("member", "tile", None, None)
    in_specs = (field,) * 6 + (P("tile"), P("tile"), P("tile"), P("tile", None))
    out_specs = (field, P("member", "tile", None), P("member", None))
    run = functools.partial(body, mesh.shape["tile"], mesh.shape["member"])
    return jax.shard_map(run, mesh=mesh, in_specs=in_specs, out_specs=out_specs, check_vma=False)
```

time: 75.5 us -> 24.9 us (0.33)
  blocking collectives: 34.7 us -> 0 us
  Pallas kernels: 0 us -> 21.2 us
  starting transfers between devices: 20.7 us -> 0 us
  local copies, waits for them, and re-layouts: 12.9 us -> 2.86 us
  other arithmetic: 3.37 us -> 0 us
  waiting for transfers between devices: 1.85 us -> 0 us
    pallas_call x0 -> x1, Pallas kernels: none -> 21.2 us  [body(): pl.pallas_call(functools.partial(kernel, tiles, members), out_shape=(jax....]
    ppermute x8 -> x0, starting transfers between devices: 20.7 us -> none  [the longest x4 15.5 us: with_halo(): lax.ppermute(tail, axis, [(i, (i + 1) % count) for i in range(ends)])]
    all_gather x1 -> x0, blocking collectives: 20.7 us -> none  [body(): gathered = lax.all_gather(scaled, 'member', axis=0, tiled=True)]
    psum x2 -> x0, blocking collectives: 14 us -> none  [the longest x1 8.4 us: body(): lax.psum(jnp.dot(onehot, table, precision=lax.Precision.HIGHEST), 'tile')]
    gather x4 -> x0, local copies, waits for them, and re-layouts: 6.89 us -> none  [the longest x3 5.17 us: body(): picked = jnp.take(state.reshape(members, -1), conn_cell, axis=1)]
    ppermute x8 -> x0, waiting for transfers between devices: 1.85 us -> none  [the longest x4 1.84 us: with_halo(): lax.ppermute(head, axis, [((i + 1) % count, i) for i in range(ends)])]
    unnamed x24 -> x7, local copies, waits for them, and re-layouts: 4.6 us -> 2.86 us
    slice x15 -> x0, local copies, waits for them, and re-layouts: 1.35 us -> none  [the longest x1 0.78 us: with_halo(): head = lax.slice_in_dim(cells, 0, width, axis=dim)]
  transfers between devices with their start and end apart: 8 -> 0, of which waited for: 2 -> 0; matrix products, arithmetic and copies ran while one was open for 8% -> 0% of each run, Pallas kernels for 0% -> 0%
where the time goes in v1:
time: 24.9 us; the launch traced here: 24.8 us
  Pallas kernels  21.2 us (85%)
  local copies, waits for them, and re-layouts  2.86 us (11%)
  between operations  0.65 us (3%)
    pallas_call x1, Pallas kernels, body(): pl.pallas_call(functools.partial(kernel, tiles, members), out_shape=(jax....  21.2 us
    unnamed x7, local copies, waits for them, and re-layouts  2.86 us

profile of v1, /device:TPU:0, one launch (start us, length us, event | category | flops | bytes accessed | tf_op | source)
XLA Modules:
  0.0 24.8 jit_solution(3968056637417084930)
XLA Ops:
  0.6 21.2 %transport.1 = (f32[1,8,64,128]{3,2,1,0:T(8,128)}, f32[3,1,8]{2,1,0:T(1,128)}, f32[1,8]{1,0:T(1,128)}) custom-call(f32[1,8,64,128]{3,2,1,0:T(8,128)} %sat_hbm.1, f32[1,8,64,128]{3,2,1,0:T(8,128)} %mob_hbm.1, f32[1,8,64,128]{3,2,1,0:T(8,128)} %pore_hbm.1, f32[1,8,64,128]{3,2,1,0:T(8,128)} %qx_hbm.1, f32[1,8,64,128]{3,2,1,0:T(8,128)} %qy_hbm.1, ...), custom_call_target="tpu_custom_call" | custom-call | flops 19660800 | bytes 1835008 | tf_op jit(solution)/shard_map/transport/pallas_call | solution.py:357
  21.9 0.0 copy-start
  21.9 1.7 %copy.16 = f32[1,8,64,128]{3,2,1,0:T(8,128)} copy(f32[1,8,64,128]{3,2,1,0:T(8,128)} %get-tuple-element.12) | data formatting | bytes 524288
  23.6 0.0 copy-done
  23.6 0.0 copy-start.1
  23.6 0.6 %copy.17 = f32[1,8,3]{1,0,2:T(1,128)} copy(f32[1,8,3]{1,0,2:T(1,128)S(1)} %bitcast.6) | data formatting | bytes 192
  24.1 0.1 copy-done.1
  24.3 0.5 %copy.18 = f32[1,8]{1,0:T(1,128)} copy(f32[1,8]{1,0:T(1,128)S(1)} %copy-done.1) | data formatting | bytes 64
Async XLA Ops:
  21.9 1.7 %copy-start = (f32[3,1,8]{2,1,0:T(1,128)S(1)}, f32[3,1,8]{2,1,0:T(1,128)}, u32[]{:S(2)}) copy-start(f32[3,1,8]{2,1,0:T(1,128)} %get-tuple-element.7) | copy-start | bytes 292
  23.6 0.7 %copy-start.1 = (f32[1,8]{1,0:T(1,128)S(1)}, f32[1,8]{1,0:T(1,128)}, u32[]{:S(2)}) copy-start(f32[1,8]{1,0:T(1,128)} %get-tuple-element.14) | copy-start | bytes 100

commit v2 on v1

--- a/solution.py
+++ b/solution.py
@@ -11,6 +11,8 @@
 LANES = 128
 SUBLANES = 8
 MESH = pl.DeviceIdType.MESH
+RUN_VMEM = 60 * 1024 * 1024
+OUT_VMEM = 4 * 1024 * 1024
 
 
 def frac(sat, mob):
@@ -41,8 +43,8 @@
     factor_hbm,
     obs_hbm,
     new_ref,
-    rates_ref,
-    gram_ref,
+    whole_ref,
+    data,
     sat,
     mob,
     pore,
@@ -63,7 +65,6 @@
     well_mask,
     obs_all,
     sums,
-    data,
     in_sem,
     halo_send,
     halo_recv,
@@ -89,8 +90,12 @@
         pltpu.make_async_copy(src, dst, in_sem.at[n])
         for n, (src, dst) in enumerate(
             (
-                (sat_hbm.at[0], sat),
-                (mob_hbm.at[0], mob),
+                (sat_hbm.at[0, 0], sat.at[0]),
+                (mob_hbm.at[0, 0], mob.at[0]),
+                (sat_hbm.at[0, last], sat.at[last]),
+                (mob_hbm.at[0, last], mob.at[last]),
+                (sat_hbm.at[0, 1:last], sat.at[1:last]),
+                (mob_hbm.at[0, 1:last], mob.at[1:last]),
                 (qx_hbm.at[0], qx),
                 (qz_hbm.at[0], qz),
                 (qy_hbm.at[0], qy),
@@ -179,12 +184,13 @@
 
     def set_split(i, value):
         high = value.astype(jnp.bfloat16)
-        at = pl.ds(pl.multiple_of(i * layers, layers), layers)
+        place = {0: 0, last: 1}[i] if isinstance(i, int) else i + 1
+        at = pl.ds(pl.multiple_of(place * layers, layers), layers)
         split[at, 0:columns] = high
         split[at, columns : 2 * columns] = (value - high.astype(jnp.float32)).astype(jnp.bfloat16)
 
-    loads[0].wait()
-    loads[1].wait()
+    for load in loads[0:4]:
+        load.wait()
     set_flow(0, 0, frac(sat[0], mob[0]))
     set_flow(0, last, frac(sat[last], mob[last]))
     send_halo(0)
@@ -193,7 +199,7 @@
     def _():
         q_copy.start()
 
-    loads[6].wait()
+    loads[10].wait()
     obs_all[tile] = jnp.ones((SUBLANES, LANES), jnp.float32)
     obs_all[tile, 0:SUBSTEPS, 0:wells_dev] = obs_ref[...]
     obs_copies = exchange(obs_all.at[tile], obs_all.at[tile], tiles, "tile", tile, obs_send, obs_recv)
@@ -202,8 +208,10 @@
         set_flow(0, i, frac(sat[i], mob[i]))
         return carry
 
+    for load in loads[4:6]:
+        load.wait()
     lax.fori_loop(1, last, first_flow, 0, unroll=True)
-    for load in loads[2:6]:
+    for load in loads[6:10]:
         load.wait()
 
     col_ids = lax.broadcasted_iota(jnp.int32, (layers, columns), 1)
@@ -228,14 +236,16 @@
         set_split(i, value)
 
     def set_masks():
-        for load in loads[7:]:
+        for load in loads[11:]:
             load.wait()
         lane_ids = lax.broadcasted_iota(jnp.int32, (conns, LANES), 1)
         cell_col = columns_of(cell_ref[...])
         row_col = lax.shift_right_logical(cell_col, columns.bit_length() - 1)
+        spot = jnp.where(row_col < layers, row_col, row_col + layers)
+        spot = jnp.where(row_col < last * layers, spot, row_col - (last - 1) * layers)
         for b in range(rows * layers // LANES):
             pick[:, b * LANES : (b + 1) * LANES] = jnp.where(
-                row_col == lane_ids + b * LANES, 1.0, 0.0
+                spot == lane_ids + b * LANES, 1.0, 0.0
             ).astype(jnp.bfloat16)
         lane_mask[...] = jnp.where(
             cell_col - row_col * columns == lane_ids, columns_of(factor_ref[...]), 0.0
@@ -243,7 +253,22 @@
         well_mask[...] = jnp.where(columns_of(well_ref[...]) == lane_ids, 1.0, 0.0)
 
     step_rates = []
+    edge = 2 * layers
+
+    def gather(start, stop):
+        found = jnp.dot(
+            pick[:, start:stop], split[start:stop, :], preferred_element_type=jnp.float32
+        )
+        return found[:, 0:columns] + found[:, columns : 2 * columns]
+
+    def add_rates(found):
+        rate = jnp.sum(found * lane_mask[...], axis=1, keepdims=True) * well_mask[...]
+        step_rates.append(jnp.sum(rate, axis=0, keepdims=True))
+
     for k in range(SUBSTEPS):
+        if k > 0:
+            add_rates(gather(0, rows * layers))
+
         def inner(i, face_lo, k=k):
             face_hi = face(qx[i + 1], flow[k, i], flow[k, i + 1])
             update(k, i, face_lo, face_hi)
@@ -253,6 +278,8 @@
         face_last = lax.fori_loop(1, last, inner, face_one, unroll=True)
         if k == 0:
             set_masks()
+        if k + 1 == SUBSTEPS:
+            found_inner = gather(edge, rows * layers)
 
         down, up = halos[k]
 
@@ -281,11 +308,7 @@
         update(k, last, face_last, face(q_above[...], flow[k, last], above))
         if k + 1 < SUBSTEPS:
             send_halo(k + 1)
-        found = jnp.dot(pick[...], split[...], preferred_element_type=jnp.float32)
-        found = (found[:, 0:columns] + found[:, columns : 2 * columns]) * lane_mask[...]
-        rate = jnp.sum(found, axis=1, keepdims=True) * well_mask[...]
-        step_rates.append(jnp.sum(rate, axis=0, keepdims=True))
-
+    add_rates(found_inner + gather(0, edge))
     step_rates.append(jnp.zeros((SUBLANES - SUBSTEPS, LANES), jnp.float32))
     sums[tile] = jnp.concatenate(step_rates, axis=0)
     sum_copies = exchange(sums.at[tile], sums.at[tile], tiles, "tile", tile, sum_send, sum_recv)
@@ -305,12 +328,40 @@
     data_copies = exchange(
         data.at[member], data.at[member], members, "member", member, data_send, data_recv
     )
-    mine = pltpu.roll(whole, lax.rem(LANES - tile * wells_dev, LANES), 1)
-    for k in range(SUBSTEPS):
-        rates_ref[k] = mine[k : k + 1, 0:wells_dev]
-
+    whole_ref[...] = whole
     for copy in data_copies:
         copy.wait_recv()
+
+    for down, up in halos:
+
+        @pl.when(has_lo)
+        def _():
+            down.wait_send()
+
+        @pl.when(has_hi)
+        def _():
+            up.wait_send()
+
+    @pl.when(has_lo)
+    def _():
+        q_copy.wait_send()
+
+    for copy in obs_copies + sum_copies + data_copies:
+        copy.wait_send()
+
+
+def finish(new_ref, whole_ref, data, new_hbm, rates_hbm, gram_hbm, rates, gram, out_sem):
+    tile = lax.axis_index("tile")
+    member = lax.axis_index("member")
+    members = data.shape[0]
+    wells_dev = rates.shape[2]
+    new_out = pltpu.make_async_copy(new_ref, new_hbm, out_sem.at[0])
+    new_out.start()
+    mine = pltpu.roll(whole_ref[...], lax.rem(LANES - tile * wells_dev, LANES), 1)
+    for k in range(SUBSTEPS):
+        rates[k] = mine[k : k + 1, 0:wells_dev]
+    rates_out = pltpu.make_async_copy(rates, rates_hbm, out_sem.at[1])
+    rates_out.start()
     mean = data[0]
     for m in range(1, members):
         mean = mean + data[m]
@@ -325,24 +376,12 @@
         jnp.int32, square, 1
     )
     line = jnp.sum(jnp.where(diagonal, terms, 0.0), axis=0, keepdims=True)
-    gram_ref[...] = line[:, 0:members] / (members - 1.0)
-
-    for down, up in halos:
-
-        @pl.when(has_lo)
-        def _():
-            down.wait_send()
-
-        @pl.when(has_hi)
-        def _():
-            up.wait_send()
-
-    @pl.when(has_lo)
-    def _():
-        q_copy.wait_send()
-
-    for copy in obs_copies + sum_copies + data_copies:
-        copy.wait_send()
+    gram[...] = line[:, 0:members] / (members - 1.0)
+    gram_out = pltpu.make_async_copy(gram, gram_hbm, out_sem.at[2])
+    gram_out.start()
+    new_out.wait()
+    rates_out.wait()
+    gram_out.wait()
 
 
 def body(tiles, members, sat, mob, pore, qx, qy, qz, cell, well, factor, obs):
@@ -354,12 +393,12 @@
     dma = pltpu.SemaphoreType.DMA
     hbm_spec = pl.BlockSpec(memory_space=pltpu.HBM)
     vmem_spec = pl.BlockSpec(memory_space=pltpu.VMEM)
-    new, rates, gram = pl.pallas_call(
+    new, whole, data = pl.pallas_call(
         functools.partial(kernel, tiles, members),
         out_shape=(
-            jax.ShapeDtypeStruct(sat.shape, f32),
-            jax.ShapeDtypeStruct((SUBSTEPS, 1, wells_dev), f32),
-            jax.ShapeDtypeStruct((1, members), f32),
+            pltpu.VMEM(sat.shape, f32),
+            pltpu.VMEM((SUBLANES, LANES), f32),
+            pltpu.VMEM((members, SUBLANES, LANES), f32),
         ),
         in_specs=[hbm_spec] * 10,
         out_specs=(vmem_spec,) * 3,
@@ -379,8 +418,7 @@
             pltpu.VMEM((conns, LANES), f32),
             pltpu.VMEM((tiles, SUBLANES, LANES), f32),
             pltpu.VMEM((tiles, SUBLANES, LANES), f32),
-            pltpu.VMEM((members, SUBLANES, LANES), f32),
-            dma((10,)),
+            dma((14,)),
             dma((SUBSTEPS, 2)),
             dma((SUBSTEPS, 2)),
             dma(()),
@@ -393,7 +431,7 @@
             dma((members - 1,)),
         ],
         compiler_params=pltpu.CompilerParams(
-            collective_id=0, has_side_effects=True, vmem_limit_bytes=60 * 1024 * 1024
+            collective_id=0, has_side_effects=True, vmem_limit_bytes=RUN_VMEM
         ),
         cost_estimate=pl.CostEstimate(
             flops=100 * SUBSTEPS * rows * layers * columns,
@@ -402,6 +440,23 @@
         ),
         name="transport",
     )(sat, mob, pore, qx, qy, qz, cell.reshape(1, -1), well.reshape(1, -1), factor.reshape(1, -1), obs.T)
+    new, rates, gram = pl.pallas_call(
+        finish,
+        out_shape=(
+            jax.ShapeDtypeStruct(sat.shape, f32),
+            jax.ShapeDtypeStruct((SUBSTEPS, 1, wells_dev), f32),
+            jax.ShapeDtypeStruct((1, members), f32),
+        ),
+        in_specs=[vmem_spec] * 3,
+        out_specs=(hbm_spec,) * 3,
+        scratch_shapes=[
+            pltpu.VMEM((SUBSTEPS, 1, wells_dev), f32),
+            pltpu.VMEM((1, members), f32),
+            dma((3,)),
+        ],
+        compiler_params=pltpu.CompilerParams(vmem_limit_bytes=OUT_VMEM),
+        name="finish",
+    )(new, whole, data)
     return new, jnp.transpose(rates, (1, 2, 0)), gram
 
 

time: 24.9 us -> 22 us (0.88)
  local copies, waits for them, and re-layouts: 2.86 us -> 0 us
    unnamed x7 -> x0, local copies, waits for them, and re-layouts: 2.86 us -> none
    pallas_call x1 -> x2, Pallas kernels: 21.2 us -> 21.2 us  [the longest x1 20.4 us: body(): pl.pallas_call(functools.partial(kernel, tiles, members), out_shape=(pltp...]
where the time goes in v2:
time: 22 us; the launch traced here: 21.8 us
  Pallas kernels  21.2 us (96%)
  between operations  0.64 us (3%)
    pallas_call x1, Pallas kernels, body(): pl.pallas_call(functools.partial(kernel, tiles, members), out_shape=(pltp...  20.4 us
    pallas_call x1, Pallas kernels, body(): pl.pallas_call(finish, out_shape=(jax.ShapeDtypeStruct(sat.shape, f32), j...  0.75 us

profile of v2, /device:TPU:0, one launch (start us, length us, event | category | flops | bytes accessed | tf_op | source)
XLA Modules:
  0.0 21.8 jit_solution(3351090180545353552)
XLA Ops:
  0.6 20.4 %transport.1 = (f32[1,8,64,128]{3,2,1,0:T(8,128)S(1)}, f32[8,128]{1,0:T(8,128)S(1)}, f32[8,8,128]{2,1,0:T(8,128)S(1)}) custom-call(f32[1,8,64,128]{3,2,1,0:T(8,128)} %sat_hbm.1, f32[1,8,64,128]{3,2,1,0:T(8,128)} %mob_hbm.1, f32[1,8,64,128]{3,2,1,0:T(8,128)} %pore_hbm.1, f32[1,8,64,128]{3,2,1,0:T(8,128)} %qx_hbm.1, f32[1,8,64,128]{3,2,1,0:T(8,128)} %qy_hbm.1, ...), custom_call_target="tpu_custom_call" | custom-call | flops 19660800 | bytes 1835008 | tf_op jit(solution)/shard_map/transport/pallas_call | solution.py:396
  21.1 0.7 %finish.1 = (f32[1,8,64,128]{3,2,1,0:T(8,128)}, f32[3,1,8]{2,1,0:T(1,128)}, f32[1,8]{1,0:T(1,128)}) custom-call(f32[1,8,64,128]{3,2,1,0:T(8,128)S(1)} %get-tuple-element.9.new_ref, f32[8,128]{1,0:T(8,128)S(1)} %get-tuple-element.10.whole_ref, f32[8,8,128]{2,1,0:T(8,128)S(1)} %get-tuple-element.11.data), custom_call_target="tpu_custom_call" | custom-call | tf_op jit(solution)/shard_map/finish/pallas_call | solution.py:443

commit v3 on v2

--- a/solution.py
+++ b/solution.py
@@ -18,7 +18,9 @@
 def frac(sat, mob):
     wet = sat * sat
     rest = 1.0 - sat
-    return wet / (wet + mob * (rest * rest))
+    whole = wet + mob * (rest * rest)
+    inverse = pl.reciprocal(whole, approx=True)
+    return wet * (inverse * (2.0 - whole * inverse))
 
 
 def face(flux, below, here):
@@ -59,6 +61,7 @@
     halo_lo,
     halo_hi,
     q_above,
+    partial,
     split,
     pick,
     lane_mask,
@@ -86,6 +89,16 @@
     has_lo = tile > 0
     has_hi = tile < tiles - 1
 
+    barrier = pltpu.get_barrier_semaphore()
+    for d in range(1, tiles):
+        pl.semaphore_signal(
+            barrier, inc=1, device_id={"tile": lax.rem(tile + d, tiles)}, device_id_type=MESH
+        )
+    for d in range(1, members):
+        pl.semaphore_signal(
+            barrier, inc=1, device_id={"member": lax.rem(member + d, members)}, device_id_type=MESH
+        )
+
     loads = [
         pltpu.make_async_copy(src, dst, in_sem.at[n])
         for n, (src, dst) in enumerate(
@@ -110,16 +123,6 @@
     for load in loads:
         load.start()
 
-    barrier = pltpu.get_barrier_semaphore()
-    for d in range(1, tiles):
-        pl.semaphore_signal(
-            barrier, inc=1, device_id={"tile": lax.rem(tile + d, tiles)}, device_id_type=MESH
-        )
-    for d in range(1, members):
-        pl.semaphore_signal(
-            barrier, inc=1, device_id={"member": lax.rem(member + d, members)}, device_id_type=MESH
-        )
-
     pl.semaphore_wait(barrier, tiles + members - 2)
 
     def exchange(src, dst_at, peers, axis, me, send_sem, recv_sem):
@@ -210,30 +213,31 @@
 
     for load in loads[4:6]:
         load.wait()
-    lax.fori_loop(1, last, first_flow, 0, unroll=True)
+    lax.fori_loop(1, last, first_flow, 0)
     for load in loads[6:10]:
         load.wait()
 
     col_ids = lax.broadcasted_iota(jnp.int32, (layers, columns), 1)
     lay_ids = lax.broadcasted_iota(jnp.int32, (layers, columns), 0)
 
-    def update(k, i, face_lo, face_hi):
+    def spread(k, i):
         here = flow[k, i]
         qz_i = jnp.where(lay_ids > 0, qz[i], 0.0)
         qy_i = jnp.where(col_ids > 0, qy[i], 0.0)
         face_z = face(qz_i, pltpu.roll(here, 1, 0), here)
         face_y = face(qy_i, pltpu.roll(here, 1, 1), here)
-        total = face_hi - face_lo
-        total = total + (pltpu.roll(face_z, layers - 1, 0) - face_z)
-        total = total + (pltpu.roll(face_y, columns - 1, 1) - face_y)
-        after = sat[i] - pore[i] * total
+        return (pltpu.roll(face_z, layers - 1, 0) - face_z) + (
+            pltpu.roll(face_y, columns - 1, 1) - face_y
+        )
+
+    def store(k, i, after):
         if k + 1 < SUBSTEPS:
             sat[i] = after
         else:
             new_ref[0, i] = after
         value = frac(after, mob[i])
         set_flow(k + 1, i, value)
-        set_split(i, value)
+        return value
 
     def set_masks():
         for load in loads[11:]:
@@ -271,11 +275,14 @@
 
         def inner(i, face_lo, k=k):
             face_hi = face(qx[i + 1], flow[k, i], flow[k, i + 1])
-            update(k, i, face_lo, face_hi)
+            after = sat[i] - pore[i] * ((face_hi - face_lo) + spread(k, i))
+            set_split(i, store(k, i, after))
             return face_hi
 
         face_one = face(qx[1], flow[k, 0], flow[k, 1])
-        face_last = lax.fori_loop(1, last, inner, face_one, unroll=True)
+        face_last = lax.fori_loop(1, last, inner, face_one)
+        partial[0] = sat[0] - pore[0] * (face_one + spread(k, 0))
+        partial[1] = sat[last] - pore[last] * (spread(k, last) - face_last)
         if k == 0:
             set_masks()
         if k + 1 == SUBSTEPS:
@@ -304,10 +311,12 @@
         below = jnp.where(has_lo, halo_lo[k], 0.0)
         above = jnp.where(has_hi, halo_hi[k], 0.0)
         qx_first = jnp.where(has_lo, qx[0], 0.0)
-        update(k, 0, face(qx_first, below, flow[k, 0]), face_one)
-        update(k, last, face_last, face(q_above[...], flow[k, last], above))
+        value_first = store(k, 0, partial[0] + pore[0] * face(qx_first, below, flow[k, 0]))
+        value_last = store(k, last, partial[1] - pore[last] * face(q_above[...], flow[k, last], above))
         if k + 1 < SUBSTEPS:
             send_halo(k + 1)
+        set_split(0, value_first)
+        set_split(last, value_last)
     add_rates(found_inner + gather(0, edge))
     step_rates.append(jnp.zeros((SUBLANES - SUBSTEPS, LANES), jnp.float32))
     sums[tile] = jnp.concatenate(step_rates, axis=0)
@@ -412,6 +421,7 @@
             pltpu.VMEM((SUBSTEPS, layers, columns), f32),
             pltpu.VMEM((SUBSTEPS, layers, columns), f32),
             pltpu.VMEM((layers, columns), f32),
+            pltpu.VMEM((2, layers, columns), f32),
             pltpu.VMEM((rows * layers, 2 * columns), jnp.bfloat16),
             pltpu.VMEM((conns, rows * layers), jnp.bfloat16),
             pltpu.VMEM((conns, LANES), f32),

time: 22 us -> 21.6 us (0.982)
  Pallas kernels: 21.2 us -> 20.8 us
    pallas_call x1, Pallas kernels: 20.4 us -> 20 us  [body(): pl.pallas_call(functools.partial(kernel, tiles, members), out_shape=(pltp...]
where the time goes in v3:
time: 21.6 us; the launch traced here: 21.4 us
  Pallas kernels  20.8 us (96%)
  between operations  0.64 us (3%)
    pallas_call x1, Pallas kernels, body(): pl.pallas_call(functools.partial(kernel, tiles, members), out_shape=(pltp...  20 us
    pallas_call x1, Pallas kernels, body(): pl.pallas_call(finish, out_shape=(jax.ShapeDtypeStruct(sat.shape, f32), j...  0.75 us

profile of v3, /device:TPU:0, one launch (start us, length us, event | category | flops | bytes accessed | tf_op | source)
XLA Modules:
  0.0 21.4 jit_solution(7395460210153046649)
XLA Ops:
  0.6 20.0 %transport.1 = (f32[1,8,64,128]{3,2,1,0:T(8,128)S(1)}, f32[8,128]{1,0:T(8,128)S(1)}, f32[8,8,128]{2,1,0:T(8,128)S(1)}) custom-call(f32[1,8,64,128]{3,2,1,0:T(8,128)} %sat_hbm.1, f32[1,8,64,128]{3,2,1,0:T(8,128)} %mob_hbm.1, f32[1,8,64,128]{3,2,1,0:T(8,128)} %pore_hbm.1, f32[1,8,64,128]{3,2,1,0:T(8,128)} %qx_hbm.1, f32[1,8,64,128]{3,2,1,0:T(8,128)} %qy_hbm.1, ...), custom_call_target="tpu_custom_call" | custom-call | flops 19660800 | bytes 1835008 | tf_op jit(solution)/shard_map/transport/pallas_call | solution.py:405
  20.7 0.7 %finish.1 = (f32[1,8,64,128]{3,2,1,0:T(8,128)}, f32[3,1,8]{2,1,0:T(1,128)}, f32[1,8]{1,0:T(1,128)}) custom-call(f32[1,8,64,128]{3,2,1,0:T(8,128)S(1)} %get-tuple-element.9.new_ref, f32[8,128]{1,0:T(8,128)S(1)} %get-tuple-element.10.whole_ref, f32[8,8,128]{2,1,0:T(8,128)S(1)} %get-tuple-element.11.data), custom_call_target="tpu_custom_call" | custom-call | tf_op jit(solution)/shard_map/finish/pallas_call | solution.py:453

commit v4 on v3

--- a/solution.py
+++ b/solution.py
@@ -45,8 +45,8 @@
     factor_hbm,
     obs_hbm,
     new_ref,
-    whole_ref,
-    data,
+    parts,
+    obs_all,
     sat,
     mob,
     pore,
@@ -66,8 +66,7 @@
     pick,
     lane_mask,
     well_mask,
-    obs_all,
-    sums,
+    obs_line,
     in_sem,
     halo_send,
     halo_recv,
@@ -75,29 +74,44 @@
     q_recv,
     obs_send,
     obs_recv,
-    sum_send,
-    sum_recv,
-    data_send,
-    data_recv,
+    part_send,
+    part_recv,
 ):
     tile = lax.axis_index("tile")
     member = lax.axis_index("member")
     rows, layers, columns = sat.shape
     last = rows - 1
     wells_dev = obs_ref.shape[1]
+    wells = wells_dev * tiles
     conns = cell_ref.shape[1]
     has_lo = tile > 0
     has_hi = tile < tiles - 1
 
     barrier = pltpu.get_barrier_semaphore()
-    for d in range(1, tiles):
-        pl.semaphore_signal(
-            barrier, inc=1, device_id={"tile": lax.rem(tile + d, tiles)}, device_id_type=MESH
-        )
-    for d in range(1, members):
-        pl.semaphore_signal(
-            barrier, inc=1, device_id={"member": lax.rem(member + d, members)}, device_id_type=MESH
-        )
+
+    def peer(dm, dt):
+        to_member = member + dm
+        to_tile = tile + dt
+        return {
+            "member": jnp.where(to_member >= members, to_member - members, to_member),
+            "tile": jnp.where(to_tile >= tiles, to_tile - tiles, to_tile),
+        }
+
+    def for_peers(act):
+        for dt in range(1, tiles):
+            act(0, dt)
+
+        def far(dm, carry):
+            for dt in range(tiles):
+                act(dm, dt)
+            return carry
+
+        lax.fori_loop(1, members, far, 0)
+
+    def greet(dm, dt):
+        pl.semaphore_signal(barrier, inc=1, device_id=peer(dm, dt), device_id_type=MESH)
+
+    for_peers(greet)
 
     loads = [
         pltpu.make_async_copy(src, dst, in_sem.at[n])
@@ -123,7 +137,7 @@
     for load in loads:
         load.start()
 
-    pl.semaphore_wait(barrier, tiles + members - 2)
+    pl.semaphore_wait(barrier, tiles * members - 1)
 
     def exchange(src, dst_at, peers, axis, me, send_sem, recv_sem):
         copies = []
@@ -203,8 +217,16 @@
         q_copy.start()
 
     loads[10].wait()
-    obs_all[tile] = jnp.ones((SUBLANES, LANES), jnp.float32)
-    obs_all[tile, 0:SUBSTEPS, 0:wells_dev] = obs_ref[...]
+    obs_line[...] = jnp.zeros_like(obs_line)
+    obs_line[0:SUBSTEPS, 0:wells_dev] = obs_ref[...]
+    lines = [jnp.zeros((1, LANES), jnp.float32)] * parts.shape[2]
+    for k in range(SUBSTEPS):
+        row, lane = divmod(k * wells, LANES)
+        lines[row] = lines[row] + pltpu.roll(
+            obs_line[k : k + 1, :], lane + tile * wells_dev, 1
+        )
+    packed = jnp.concatenate(lines, axis=0)
+    obs_all[tile] = jnp.where(packed == 0.0, 1.0, packed)
     obs_copies = exchange(obs_all.at[tile], obs_all.at[tile], tiles, "tile", tile, obs_send, obs_recv)
 
     def first_flow(i, carry):
@@ -318,28 +340,27 @@
         set_split(0, value_first)
         set_split(last, value_last)
     add_rates(found_inner + gather(0, edge))
-    step_rates.append(jnp.zeros((SUBLANES - SUBSTEPS, LANES), jnp.float32))
-    sums[tile] = jnp.concatenate(step_rates, axis=0)
-    sum_copies = exchange(sums.at[tile], sums.at[tile], tiles, "tile", tile, sum_send, sum_recv)
+    lines = [jnp.zeros((1, LANES), jnp.float32)] * parts.shape[2]
+    for k in range(SUBSTEPS):
+        row, lane = divmod(k * wells, LANES)
+        lines[row] = lines[row] + (pltpu.roll(step_rates[k], lane, 1) if lane else step_rates[k])
+    parts[tile, member] = jnp.concatenate(lines, axis=0)
+
+    def part_copy(dm, dt):
+        n = dm * tiles + dt - 1
+        return pltpu.make_async_remote_copy(
+            src_ref=parts.at[tile, member],
+            dst_ref=parts.at[tile, member],
+            send_sem=part_send.at[n],
+            recv_sem=part_recv.at[n],
+            device_id=peer(dm, dt),
+            device_id_type=MESH,
+        )
+
+    for_peers(lambda dm, dt: part_copy(dm, dt).start())
     for copy in obs_copies:
         copy.wait_recv()
-    lane_row = lax.broadcasted_iota(jnp.int32, (SUBLANES, LANES), 1)
-    obs_whole = obs_all[0]
-    for t in range(1, tiles):
-        moved = pltpu.roll(obs_all[t], t * wells_dev, 1)
-        obs_whole = jnp.where(lane_row >= t * wells_dev, moved, obs_whole)
-    for copy in sum_copies:
-        copy.wait_recv()
-    whole = sums[0]
-    for t in range(1, tiles):
-        whole = whole + sums[t]
-    data[member] = whole / obs_whole
-    data_copies = exchange(
-        data.at[member], data.at[member], members, "member", member, data_send, data_recv
-    )
-    whole_ref[...] = whole
-    for copy in data_copies:
-        copy.wait_recv()
+    for_peers(lambda dm, dt: part_copy(dm, dt).wait_recv())
 
     for down, up in halos:
 
@@ -355,27 +376,44 @@
     def _():
         q_copy.wait_send()
 
-    for copy in obs_copies + sum_copies + data_copies:
+    for copy in obs_copies:
         copy.wait_send()
-
-
-def finish(new_ref, whole_ref, data, new_hbm, rates_hbm, gram_hbm, rates, gram, out_sem):
+    for_peers(lambda dm, dt: part_copy(dm, dt).wait_send())
+
+
+def finish(new_ref, parts, obs_all, new_hbm, rates_hbm, gram_hbm, rates, gram, out_sem):
     tile = lax.axis_index("tile")
     member = lax.axis_index("member")
-    members = data.shape[0]
+    tiles, members = parts.shape[0:2]
     wells_dev = rates.shape[2]
+    wells = wells_dev * tiles
     new_out = pltpu.make_async_copy(new_ref, new_hbm, out_sem.at[0])
     new_out.start()
-    mine = pltpu.roll(whole_ref[...], lax.rem(LANES - tile * wells_dev, LANES), 1)
+
+    def tile_sum(m):
+        whole = parts[0, m]
+        for t in range(1, tiles):
+            whole = whole + parts[t, m]
+        return whole
+
+    mine = tile_sum(member)
     for k in range(SUBSTEPS):
-        rates[k] = mine[k : k + 1, 0:wells_dev]
+        row, lane = divmod(k * wells, LANES)
+        moved = pltpu.roll(
+            mine[row : row + 1], lax.rem(2 * LANES - lane - tile * wells_dev, LANES), 1
+        )
+        rates[k] = moved[:, 0:wells_dev]
     rates_out = pltpu.make_async_copy(rates, rates_hbm, out_sem.at[1])
     rates_out.start()
+    obs = obs_all[0]
+    for t in range(1, tiles):
+        obs = obs * obs_all[t]
+    data = [tile_sum(m) / obs for m in range(members)]
     mean = data[0]
     for m in range(1, members):
         mean = mean + data[m]
     mean = mean * (1.0 / members)
-    own = data[member] - mean
+    own = mine / obs - mean
     terms = jnp.concatenate(
         [jnp.sum(own * (data[m] - mean), axis=0, keepdims=True) for m in range(members)], axis=0
     )
@@ -402,12 +440,13 @@
     dma = pltpu.SemaphoreType.DMA
     hbm_spec = pl.BlockSpec(memory_space=pltpu.HBM)
     vmem_spec = pl.BlockSpec(memory_space=pltpu.VMEM)
-    new, whole, data = pl.pallas_call(
+    lines = -(-SUBSTEPS * wells_dev * tiles // LANES)
+    new, parts, obs_all = pl.pallas_call(
         functools.partial(kernel, tiles, members),
         out_shape=(
             pltpu.VMEM(sat.shape, f32),
-            pltpu.VMEM((SUBLANES, LANES), f32),
-            pltpu.VMEM((members, SUBLANES, LANES), f32),
+            pltpu.VMEM((tiles, members, lines, LANES), f32),
+            pltpu.VMEM((tiles, lines, LANES), f32),
         ),
         in_specs=[hbm_spec] * 10,
         out_specs=(vmem_spec,) * 3,
@@ -426,8 +465,7 @@
             pltpu.VMEM((conns, rows * layers), jnp.bfloat16),
             pltpu.VMEM((conns, LANES), f32),
             pltpu.VMEM((conns, LANES), f32),
-            pltpu.VMEM((tiles, SUBLANES, LANES), f32),
-            pltpu.VMEM((tiles, SUBLANES, LANES), f32),
+            pltpu.VMEM((SUBLANES, LANES), f32),
             dma((14,)),
             dma((SUBSTEPS, 2)),
             dma((SUBSTEPS, 2)),
@@ -435,10 +473,8 @@
             dma(()),
             dma((tiles - 1,)),
             dma((tiles - 1,)),
-            dma((tiles - 1,)),
-            dma((tiles - 1,)),
-            dma((members - 1,)),
-            dma((members - 1,)),
+            dma((tiles * members - 1,)),
+            dma((tiles * members - 1,)),
         ],
         compiler_params=pltpu.CompilerParams(
             collective_id=0, has_side_effects=True, vmem_limit_bytes=RUN_VMEM
@@ -466,7 +502,7 @@
         ],
         compiler_params=pltpu.CompilerParams(vmem_limit_bytes=OUT_VMEM),
         name="finish",
-    )(new, whole, data)
+    )(new, parts, obs_all)
     return new, jnp.transpose(rates, (1, 2, 0)), gram
 
 

time: 21.6 us -> 20.2 us (0.935)
  Pallas kernels: 20.8 us -> 19.4 us
    pallas_call x1, Pallas kernels: 20 us -> 18.7 us  [body(): pl.pallas_call(functools.partial(kernel, tiles, members), out_shape=(pltp...]
where the time goes in v4:
time: 20.2 us; the launch traced here: 20 us
  Pallas kernels  19.4 us (96%)
  between operations  0.64 us (3%)
    pallas_call x1, Pallas kernels, body(): pl.pallas_call(functools.partial(kernel, tiles, members), out_shape=(pltp...  18.7 us
    pallas_call x1, Pallas kernels, body(): pl.pallas_call(finish, out_shape=(jax.ShapeDtypeStruct(sat.shape, f32), j...  0.75 us

profile of v4, /device:TPU:0, one launch (start us, length us, event | category | flops | bytes accessed | tf_op | source)
XLA Modules:
  0.0 20.0 jit_solution(2165290612243906110)
XLA Ops:
  0.6 18.7 %transport.1 = (f32[1,8,64,128]{3,2,1,0:T(8,128)S(1)}, f32[4,8,1,128]{3,2,1,0:T(1,128)S(1)}, f32[4,1,128]{2,1,0:T(1,128)S(1)}) custom-call(f32[1,8,64,128]{3,2,1,0:T(8,128)} %sat_hbm.1, f32[1,8,64,128]{3,2,1,0:T(8,128)} %mob_hbm.1, f32[1,8,64,128]{3,2,1,0:T(8,128)} %pore_hbm.1, f32[1,8,64,128]{3,2,1,0:T(8,128)} %qx_hbm.1, f32[1,8,64,128]{3,2,1,0:T(8,128)} %qy_hbm.1, ...), custom_call_target="tpu_custom_call" | custom-call | flops 19660800 | bytes 1835008 | tf_op jit(solution)/shard_map/transport/pallas_call | solution.py:444
  19.3 0.7 %finish.1 = (f32[1,8,64,128]{3,2,1,0:T(8,128)}, f32[3,1,8]{2,1,0:T(1,128)}, f32[1,8]{1,0:T(1,128)}) custom-call(f32[1,8,64,128]{3,2,1,0:T(8,128)S(1)} %get-tuple-element.9.new_ref, f32[4,8,1,128]{3,2,1,0:T(1,128)S(1)} %get-tuple-element.10.parts, f32[4,1,128]{2,1,0:T(1,128)S(1)} %get-tuple-element.11.obs_all), custom_call_target="tpu_custom_call" | custom-call | tf_op jit(solution)/shard_map/finish/pallas_call | solution.py:489

commit v5 on v4

--- a/solution.py
+++ b/solution.py
@@ -58,8 +58,12 @@
     factor_ref,
     obs_ref,
     flow,
-    halo_lo,
-    halo_hi,
+    beside,
+    behind,
+    sat_beside,
+    sat_edge,
+    fixed,
+    q_below,
     q_above,
     partial,
     split,
@@ -70,8 +74,6 @@
     in_sem,
     halo_send,
     halo_recv,
-    q_send,
-    q_recv,
     obs_send,
     obs_recv,
     part_send,
@@ -155,66 +157,74 @@
             copies[-1].start()
         return copies
 
-    q_copy = pltpu.make_async_remote_copy(
-        src_ref=qx_hbm.at[0, 0],
-        dst_ref=q_above,
-        send_sem=q_send,
-        recv_sem=q_recv,
-        device_id={"tile": jnp.maximum(tile - 1, 0)},
-        device_id_type=MESH,
-    )
-
-    def halo_copies(k):
-        down = pltpu.make_async_remote_copy(
-            src_ref=flow.at[k, 0],
-            dst_ref=halo_hi.at[k],
-            send_sem=halo_send.at[k, 0],
-            recv_sem=halo_recv.at[k, 0],
-            device_id={"tile": jnp.maximum(tile - 1, 0)},
+    def to_side(n, up, src, dst):
+        side = 0 if up else 1
+        beyond = jnp.minimum(tile + 1, tiles - 1) if up else jnp.maximum(tile - 1, 0)
+        return pltpu.make_async_remote_copy(
+            src_ref=src,
+            dst_ref=dst,
+            send_sem=halo_send.at[side, n],
+            recv_sem=halo_recv.at[side, n],
+            device_id={"tile": beyond},
             device_id_type=MESH,
         )
-        up = pltpu.make_async_remote_copy(
-            src_ref=flow.at[k, last],
-            dst_ref=halo_lo.at[k],
-            send_sem=halo_send.at[k, 1],
-            recv_sem=halo_recv.at[k, 1],
-            device_id={"tile": jnp.minimum(tile + 1, tiles - 1)},
-            device_id_type=MESH,
-        )
-        return down, up
-
-    halos = [halo_copies(k) for k in range(SUBSTEPS)]
-
-    def send_halo(k):
-        down, up = halos[k]
-
+
+    ups = [
+        to_side(0, True, flow.at[0, last], beside.at[0]),
+        to_side(1, True, qx_hbm.at[0, last], q_below),
+    ]
+    downs = [
+        to_side(0, False, flow.at[0, 0], beside.at[1]),
+        to_side(1, False, qx_hbm.at[0, 0:2], q_above),
+    ]
+    for n, field in enumerate((mob_hbm, pore_hbm, qz_hbm, qy_hbm)):
+        ups.append(to_side(n + 2, True, field.at[0, last], fixed.at[0, n]))
+        downs.append(to_side(n + 2, False, field.at[0, 0], fixed.at[1, n]))
+    ups.append(to_side(6, True, flow.at[1, last - 1], behind.at[0]))
+    downs.append(to_side(6, False, flow.at[1, 1], behind.at[1]))
+    ups.append(to_side(7, True, sat_edge.at[1], sat_beside.at[0]))
+    downs.append(to_side(7, False, sat_edge.at[0], sat_beside.at[1]))
+
+    def send(start, stop):
         @pl.when(has_lo)
         def _():
-            down.start()
+            for copy in downs[start:stop]:
+                copy.start()
 
         @pl.when(has_hi)
         def _():
-            up.start()
+            for copy in ups[start:stop]:
+                copy.start()
+
+    def receive(start, stop):
+        @pl.when(has_lo)
+        def _():
+            for copy in ups[start:stop]:
+                copy.wait_recv()
+
+        @pl.when(has_hi)
+        def _():
+            for copy in downs[start:stop]:
+                copy.wait_recv()
 
     def set_flow(k, i, value):
         flow[k, i] = value
 
-    def set_split(i, value):
+    def set_split(k, i, value):
         high = value.astype(jnp.bfloat16)
-        place = {0: 0, last: 1}[i] if isinstance(i, int) else i + 1
+        if isinstance(i, int):
+            place = {0: 0, last: 1, 1: 2, last - 1: 3}[i]
+        else:
+            place = jnp.where(i == 1, 2, jnp.where(i == last - 1, 3, i + 2))
         at = pl.ds(pl.multiple_of(place * layers, layers), layers)
-        split[at, 0:columns] = high
-        split[at, columns : 2 * columns] = (value - high.astype(jnp.float32)).astype(jnp.bfloat16)
+        split[k % 2, at, 0:columns] = high
+        split[k % 2, at, columns : 2 * columns] = (value - high.astype(jnp.float32)).astype(jnp.bfloat16)
 
     for load in loads[0:4]:
         load.wait()
     set_flow(0, 0, frac(sat[0], mob[0]))
     set_flow(0, last, frac(sat[last], mob[last]))
-    send_halo(0)
-
-    @pl.when(has_lo)
-    def _():
-        q_copy.start()
+    send(0, 6)
 
     loads[10].wait()
     obs_line[...] = jnp.zeros_like(obs_line)
@@ -242,15 +252,20 @@
     col_ids = lax.broadcasted_iota(jnp.int32, (layers, columns), 1)
     lay_ids = lax.broadcasted_iota(jnp.int32, (layers, columns), 0)
 
-    def spread(k, i):
-        here = flow[k, i]
-        qz_i = jnp.where(lay_ids > 0, qz[i], 0.0)
-        qy_i = jnp.where(col_ids > 0, qy[i], 0.0)
+    def spread_of(here, qz_i, qy_i):
+        qz_i = jnp.where(lay_ids > 0, qz_i, 0.0)
+        qy_i = jnp.where(col_ids > 0, qy_i, 0.0)
         face_z = face(qz_i, pltpu.roll(here, 1, 0), here)
         face_y = face(qy_i, pltpu.roll(here, 1, 1), here)
         return (pltpu.roll(face_z, layers - 1, 0) - face_z) + (
             pltpu.roll(face_y, columns - 1, 1) - face_y
         )
+
+    def spread(k, i):
+        return spread_of(flow[k, i], qz[i], qy[i])
+
+    def face_at(k, i):
+        return face(qx[i], flow[k, i - 1], flow[k, i])
 
     def store(k, i, after):
         if k + 1 < SUBSTEPS:
@@ -268,6 +283,8 @@
         cell_col = columns_of(cell_ref[...])
         row_col = lax.shift_right_logical(cell_col, columns.bit_length() - 1)
         spot = jnp.where(row_col < layers, row_col, row_col + layers)
+        spot = jnp.where(row_col < 2 * layers, spot, row_col + 2 * layers)
+        spot = jnp.where(row_col < (last - 1) * layers, spot, row_col - (last - 4) * layers)
         spot = jnp.where(row_col < last * layers, spot, row_col - (last - 1) * layers)
         for b in range(rows * layers // LANES):
             pick[:, b * LANES : (b + 1) * LANES] = jnp.where(
@@ -279,11 +296,13 @@
         well_mask[...] = jnp.where(columns_of(well_ref[...]) == lane_ids, 1.0, 0.0)
 
     step_rates = []
-    edge = 2 * layers
-
-    def gather(start, stop):
+    two = 2 * layers
+    four = 4 * layers
+    cells = rows * layers
+
+    def gather(k, start, stop):
         found = jnp.dot(
-            pick[:, start:stop], split[start:stop, :], preferred_element_type=jnp.float32
+            pick[:, start:stop], split[k % 2, start:stop, :], preferred_element_type=jnp.float32
         )
         return found[:, 0:columns] + found[:, columns : 2 * columns]
 
@@ -291,55 +310,77 @@
         rate = jnp.sum(found * lane_mask[...], axis=1, keepdims=True) * well_mask[...]
         step_rates.append(jnp.sum(rate, axis=0, keepdims=True))
 
-    for k in range(SUBSTEPS):
-        if k > 0:
-            add_rates(gather(0, rows * layers))
-
-        def inner(i, face_lo, k=k):
+    def inner_rows(k, start, stop):
+        def inner(i, face_lo):
             face_hi = face(qx[i + 1], flow[k, i], flow[k, i + 1])
-            after = sat[i] - pore[i] * ((face_hi - face_lo) + spread(k, i))
-            set_split(i, store(k, i, after))
+            value = store(k, i, sat[i] - pore[i] * ((face_hi - face_lo) + spread(k, i)))
+            set_split(k, i, value)
             return face_hi
 
-        face_one = face(qx[1], flow[k, 0], flow[k, 1])
-        face_last = lax.fori_loop(1, last, inner, face_one)
-        partial[0] = sat[0] - pore[0] * (face_one + spread(k, 0))
-        partial[1] = sat[last] - pore[last] * (spread(k, last) - face_last)
-        if k == 0:
-            set_masks()
-        if k + 1 == SUBSTEPS:
-            found_inner = gather(edge, rows * layers)
-
-        down, up = halos[k]
-
-        @pl.when(has_lo)
-        def _():
-            up.wait_recv()
-
-        @pl.when(has_hi)
-        def _():
-            down.wait_recv()
-
-        if k == 0:
-
-            @pl.when(has_hi)
-            def _():
-                q_copy.wait_recv()
-
-            @pl.when(jnp.logical_not(has_hi))
-            def _():
-                q_above[...] = jnp.zeros_like(q_above)
-
-        below = jnp.where(has_lo, halo_lo[k], 0.0)
-        above = jnp.where(has_hi, halo_hi[k], 0.0)
-        qx_first = jnp.where(has_lo, qx[0], 0.0)
-        value_first = store(k, 0, partial[0] + pore[0] * face(qx_first, below, flow[k, 0]))
-        value_last = store(k, last, partial[1] - pore[last] * face(q_above[...], flow[k, last], above))
-        if k + 1 < SUBSTEPS:
-            send_halo(k + 1)
-        set_split(0, value_first)
-        set_split(last, value_last)
-    add_rates(found_inner + gather(0, edge))
+        face_first = face_at(k, start)
+        return face_first, lax.fori_loop(start, stop, inner, face_first)
+
+    face_lo, face_hi = inner_rows(0, 1, last)
+    send(6, 7)
+    partial[0] = sat[0] - pore[0] * (face_lo + spread(0, 0))
+    partial[1] = sat[last] - pore[last] * (spread(0, last) - face_hi)
+    qx_first = jnp.where(has_lo, qx[0], 0.0)
+    set_masks()
+    receive(0, 2)
+
+    @pl.when(jnp.logical_not(has_hi))
+    def _():
+        q_above[...] = jnp.zeros_like(q_above)
+
+    below = jnp.where(has_lo, beside[0], 0.0)
+    above = jnp.where(has_hi, beside[1], 0.0)
+    first = partial[0] + pore[0] * face(qx_first, below, flow[0, 0])
+    final = partial[1] - pore[last] * face(q_above[0], flow[0, last], above)
+    sat_edge[0] = first
+    sat_edge[1] = final
+    send(7, 8)
+    set_split(0, 0, store(0, 0, first))
+    set_split(0, last, store(0, last, final))
+
+    add_rates(gather(0, 0, cells))
+    face_lo, face_hi = inner_rows(1, 1, last)
+    partial[0] = sat[0] - pore[0] * (face_lo + spread(1, 0))
+    partial[1] = sat[last] - pore[last] * (spread(1, last) - face_hi)
+    found_second = gather(1, two, cells)
+    face_lo, face_hi = inner_rows(2, 2, last - 1)
+    partial[2] = sat[1] - pore[1] * (face_lo + spread(2, 1))
+    partial[3] = sat[last - 1] - pore[last - 1] * (spread(2, last - 1) - face_hi)
+    found_third = gather(2, four, cells)
+    receive(2, 8)
+
+    def advance_beside(side, here, lower, upper):
+        mob_i, pore_i, qz_i, qy_i = (fixed[side, n] for n in range(4))
+        total = (upper - lower) + spread_of(here, qz_i, qy_i)
+        return frac(sat_beside[side] - pore_i * total, mob_i)
+
+    flow_lo = frac(sat_beside[0], fixed[0, 0])
+    flow_hi = frac(sat_beside[1], fixed[1, 0])
+    face_lo = face(qx_first, jnp.where(has_lo, flow_lo, 0.0), flow[1, 0])
+    face_hi = face(q_above[0], flow[1, last], jnp.where(has_hi, flow_hi, 0.0))
+    set_split(1, 0, store(1, 0, partial[0] + pore[0] * face_lo))
+    set_split(1, last, store(1, last, partial[1] - pore[last] * face_hi))
+    below = advance_beside(0, flow_lo, face(q_below[...], behind[0], flow_lo), face_lo)
+    above = advance_beside(1, flow_hi, face_hi, face(q_above[1], flow_hi, behind[1]))
+
+    face_lo = face(qx_first, jnp.where(has_lo, below, 0.0), flow[2, 0])
+    face_hi = face(q_above[0], flow[2, last], jnp.where(has_hi, above, 0.0))
+    face_one = face_at(2, 1)
+    face_last = face_at(2, last)
+    for i, after in (
+        (0, sat[0] - pore[0] * ((face_one - face_lo) + spread(2, 0))),
+        (1, partial[2] + pore[1] * face_one),
+        (last - 1, partial[3] - pore[last - 1] * face_last),
+        (last, sat[last] - pore[last] * ((face_hi - face_last) + spread(2, last))),
+    ):
+        set_split(2, i, store(2, i, after))
+    add_rates(found_second + gather(1, 0, two))
+    add_rates(found_third + gather(2, 0, four))
+
     lines = [jnp.zeros((1, LANES), jnp.float32)] * parts.shape[2]
     for k in range(SUBSTEPS):
         row, lane = divmod(k * wells, LANES)
@@ -362,19 +403,15 @@
         copy.wait_recv()
     for_peers(lambda dm, dt: part_copy(dm, dt).wait_recv())
 
-    for down, up in halos:
-
-        @pl.when(has_lo)
-        def _():
-            down.wait_send()
-
-        @pl.when(has_hi)
-        def _():
-            up.wait_send()
-
     @pl.when(has_lo)
     def _():
-        q_copy.wait_send()
+        for copy in downs:
+            copy.wait_send()
+
+    @pl.when(has_hi)
+    def _():
+        for copy in ups:
+            copy.wait_send()
 
     for copy in obs_copies:
         copy.wait_send()
@@ -457,20 +494,22 @@
             pltpu.VMEM((1, conns), f32),
             pltpu.VMEM((SUBSTEPS, wells_dev), f32),
             pltpu.VMEM((SUBSTEPS + 1,) + block, f32),
-            pltpu.VMEM((SUBSTEPS, layers, columns), f32),
-            pltpu.VMEM((SUBSTEPS, layers, columns), f32),
+            pltpu.VMEM((2, layers, columns), f32),
+            pltpu.VMEM((2, layers, columns), f32),
+            pltpu.VMEM((2, layers, columns), f32),
+            pltpu.VMEM((2, layers, columns), f32),
+            pltpu.VMEM((2, 4, layers, columns), f32),
             pltpu.VMEM((layers, columns), f32),
             pltpu.VMEM((2, layers, columns), f32),
-            pltpu.VMEM((rows * layers, 2 * columns), jnp.bfloat16),
+            pltpu.VMEM((4, layers, columns), f32),
+            pltpu.VMEM((2, rows * layers, 2 * columns), jnp.bfloat16),
             pltpu.VMEM((conns, rows * layers), jnp.bfloat16),
             pltpu.VMEM((conns, LANES), f32),
             pltpu.VMEM((conns, LANES), f32),
             pltpu.VMEM((SUBLANES, LANES), f32),
             dma((14,)),
-            dma((SUBSTEPS, 2)),
-            dma((SUBSTEPS, 2)),
-            dma(()),
-            dma(()),
+            dma((2, 8)),
+            dma((2, 8)),
             dma((tiles - 1,)),
             dma((tiles - 1,)),
             dma((tiles * members - 1,)),

time: 20.2 us -> 18.7 us (0.926)
  Pallas kernels: 19.4 us -> 17.9 us
    pallas_call x1, Pallas kernels: 18.7 us -> 17.1 us  [body(): pl.pallas_call(functools.partial(kernel, tiles, members), out_shape=(pltp...]
where the time goes in v5:
time: 18.7 us; the launch traced here: 18.5 us
  Pallas kernels  17.9 us (96%)
  between operations  0.64 us (3%)
    pallas_call x1, Pallas kernels, body(): pl.pallas_call(functools.partial(kernel, tiles, members), out_shape=(pltp...  17.1 us
    pallas_call x1, Pallas kernels, body(): pl.pallas_call(finish, out_shape=(jax.ShapeDtypeStruct(sat.shape, f32), j...  0.75 us

profile of v5, /device:TPU:0, one launch (start us, length us, event | category | flops | bytes accessed | tf_op | source)
XLA Modules:
  0.0 18.5 jit_solution(5037548512747034918)
XLA Ops:
  0.6 17.1 %transport.1 = (f32[1,8,64,128]{3,2,1,0:T(8,128)S(1)}, f32[4,8,1,128]{3,2,1,0:T(1,128)S(1)}, f32[4,1,128]{2,1,0:T(1,128)S(1)}) custom-call(f32[1,8,64,128]{3,2,1,0:T(8,128)} %sat_hbm.1, f32[1,8,64,128]{3,2,1,0:T(8,128)} %mob_hbm.1, f32[1,8,64,128]{3,2,1,0:T(8,128)} %pore_hbm.1, f32[1,8,64,128]{3,2,1,0:T(8,128)} %qx_hbm.1, f32[1,8,64,128]{3,2,1,0:T(8,128)} %qy_hbm.1, ...), custom_call_target="tpu_custom_call" | custom-call | flops 19660800 | bytes 1835008 | tf_op jit(solution)/shard_map/transport/pallas_call | solution.py:481
  17.8 0.7 %finish.1 = (f32[1,8,64,128]{3,2,1,0:T(8,128)}, f32[3,1,8]{2,1,0:T(1,128)}, f32[1,8]{1,0:T(1,128)}) custom-call(f32[1,8,64,128]{3,2,1,0:T(8,128)S(1)} %get-tuple-element.9.new_ref, f32[4,8,1,128]{3,2,1,0:T(1,128)S(1)} %get-tuple-element.10.parts, f32[4,1,128]{2,1,0:T(1,128)S(1)} %get-tuple-element.11.obs_all), custom_call_target="tpu_custom_call" | custom-call | tf_op jit(solution)/shard_map/finish/pallas_call | solution.py:528

commit v6 on v5

--- a/solution.py
+++ b/solution.py
@@ -100,20 +100,17 @@
         }
 
     def for_peers(act):
-        for dt in range(1, tiles):
-            act(0, dt)
-
         def far(dm, carry):
             for dt in range(tiles):
                 act(dm, dt)
             return carry
 
         lax.fori_loop(1, members, far, 0)
+        for dt in range(1, tiles):
+            act(0, dt)
 
     def greet(dm, dt):
         pl.semaphore_signal(barrier, inc=1, device_id=peer(dm, dt), device_id_type=MESH)
-
-    for_peers(greet)
 
     loads = [
         pltpu.make_async_copy(src, dst, in_sem.at[n])
@@ -136,10 +133,12 @@
             )
         )
     ]
-    for load in loads:
+    for load in loads[0:4]:
         load.start()
-
-    pl.semaphore_wait(barrier, tiles * members - 1)
+    for_peers(greet)
+    for load in loads[4:]:
+        load.start()
+
 
     def exchange(src, dst_at, peers, axis, me, send_sem, recv_sem):
         copies = []
@@ -224,6 +223,7 @@
         load.wait()
     set_flow(0, 0, frac(sat[0], mob[0]))
     set_flow(0, last, frac(sat[last], mob[last]))
+    pl.semaphore_wait(barrier, tiles * members - 1)
     send(0, 6)
 
     loads[10].wait()
@@ -326,6 +326,7 @@
     partial[1] = sat[last] - pore[last] * (spread(0, last) - face_hi)
     qx_first = jnp.where(has_lo, qx[0], 0.0)
     set_masks()
+    found_first = gather(0, two, cells)
     receive(0, 2)
 
     @pl.when(jnp.logical_not(has_hi))
@@ -342,7 +343,7 @@
     set_split(0, 0, store(0, 0, first))
     set_split(0, last, store(0, last, final))
 
-    add_rates(gather(0, 0, cells))
+    add_rates(found_first + gather(0, 0, two))
     face_lo, face_hi = inner_rows(1, 1, last)
     partial[0] = sat[0] - pore[0] * (face_lo + spread(1, 0))
     partial[1] = sat[last] - pore[last] * (spread(1, last) - face_hi)

time: 18.7 us -> 18.5 us (0.989)
  Pallas kernels: 17.9 us -> 17.7 us
where the time goes in v6:
time: 18.5 us; the launch traced here: 18.4 us
  Pallas kernels  17.7 us (96%)
  between operations  0.64 us (3%)
    pallas_call x1, Pallas kernels, body(): pl.pallas_call(functools.partial(kernel, tiles, members), out_shape=(pltp...  17 us
    pallas_call x1, Pallas kernels, body(): pl.pallas_call(finish, out_shape=(jax.ShapeDtypeStruct(sat.shape, f32), j...  0.75 us

profile of v6, /device:TPU:0, one launch (start us, length us, event | category | flops | bytes accessed | tf_op | source)
XLA Modules:
  0.0 18.4 jit_solution(10775174349098825339)
XLA Ops:
  0.6 17.0 %transport.1 = (f32[1,8,64,128]{3,2,1,0:T(8,128)S(1)}, f32[4,8,1,128]{3,2,1,0:T(1,128)S(1)}, f32[4,1,128]{2,1,0:T(1,128)S(1)}) custom-call(f32[1,8,64,128]{3,2,1,0:T(8,128)} %sat_hbm.1, f32[1,8,64,128]{3,2,1,0:T(8,128)} %mob_hbm.1, f32[1,8,64,128]{3,2,1,0:T(8,128)} %pore_hbm.1, f32[1,8,64,128]{3,2,1,0:T(8,128)} %qx_hbm.1, f32[1,8,64,128]{3,2,1,0:T(8,128)} %qy_hbm.1, ...), custom_call_target="tpu_custom_call" | custom-call | flops 19660800 | bytes 1835008 | tf_op jit(solution)/shard_map/transport/pallas_call | solution.py:482
  17.6 0.7 %finish.1 = (f32[1,8,64,128]{3,2,1,0:T(8,128)}, f32[3,1,8]{2,1,0:T(1,128)}, f32[1,8]{1,0:T(1,128)}) custom-call(f32[1,8,64,128]{3,2,1,0:T(8,128)S(1)} %get-tuple-element.9.new_ref, f32[4,8,1,128]{3,2,1,0:T(1,128)S(1)} %get-tuple-element.10.parts, f32[4,1,128]{2,1,0:T(1,128)S(1)} %get-tuple-element.11.obs_all), custom_call_target="tpu_custom_call" | custom-call | tf_op jit(solution)/shard_map/finish/pallas_call | solution.py:529

commit v7 on v6

--- a/solution.py
+++ b/solution.py
@@ -139,7 +139,6 @@
     for load in loads[4:]:
         load.start()
 
-
     def exchange(src, dst_at, peers, axis, me, send_sem, recv_sem):
         copies = []
         for d in range(1, peers):
@@ -224,8 +223,17 @@
     set_flow(0, 0, frac(sat[0], mob[0]))
     set_flow(0, last, frac(sat[last], mob[last]))
     pl.semaphore_wait(barrier, tiles * members - 1)
-    send(0, 6)
-
+    send(0, 1)
+    send(1, 2)
+
+    def first_flow(i, carry):
+        set_flow(0, i, frac(sat[i], mob[i]))
+        return carry
+
+    for load in loads[4:6]:
+        load.wait()
+    lax.fori_loop(1, last, first_flow, 0)
+    send(2, 6)
     loads[10].wait()
     obs_line[...] = jnp.zeros_like(obs_line)
     obs_line[0:SUBSTEPS, 0:wells_dev] = obs_ref[...]
@@ -238,14 +246,6 @@
     packed = jnp.concatenate(lines, axis=0)
     obs_all[tile] = jnp.where(packed == 0.0, 1.0, packed)
     obs_copies = exchange(obs_all.at[tile], obs_all.at[tile], tiles, "tile", tile, obs_send, obs_recv)
-
-    def first_flow(i, carry):
-        set_flow(0, i, frac(sat[i], mob[i]))
-        return carry
-
-    for load in loads[4:6]:
-        load.wait()
-    lax.fori_loop(1, last, first_flow, 0)
     for load in loads[6:10]:
         load.wait()
 

time: 18.5 us -> 18.5 us (level)
  no operation moved by 1% of the time
where the time goes in v7:
time: 18.5 us; the launch traced here: 18.4 us
  Pallas kernels  17.7 us (96%)
  between operations  0.64 us (3%)
    pallas_call x1, Pallas kernels, body(): pl.pallas_call(functools.partial(kernel, tiles, members), out_shape=(pltp...  17 us
    pallas_call x1, Pallas kernels, body(): pl.pallas_call(finish, out_shape=(jax.ShapeDtypeStruct(sat.shape, f32), j...  0.75 us

profile of v7, /device:TPU:0, one launch (start us, length us, event | category | flops | bytes accessed | tf_op | source)
XLA Modules:
  0.0 18.4 jit_solution(1675724266664460759)
XLA Ops:
  0.6 17.0 %transport.1 = (f32[1,8,64,128]{3,2,1,0:T(8,128)S(1)}, f32[4,8,1,128]{3,2,1,0:T(1,128)S(1)}, f32[4,1,128]{2,1,0:T(1,128)S(1)}) custom-call(f32[1,8,64,128]{3,2,1,0:T(8,128)} %sat_hbm.1, f32[1,8,64,128]{3,2,1,0:T(8,128)} %mob_hbm.1, f32[1,8,64,128]{3,2,1,0:T(8,128)} %pore_hbm.1, f32[1,8,64,128]{3,2,1,0:T(8,128)} %qx_hbm.1, f32[1,8,64,128]{3,2,1,0:T(8,128)} %qy_hbm.1, ...), custom_call_target="tpu_custom_call" | custom-call | flops 19660800 | bytes 1835008 | tf_op jit(solution)/shard_map/transport/pallas_call | solution.py:482
  17.6 0.7 %finish.1 = (f32[1,8,64,128]{3,2,1,0:T(8,128)}, f32[3,1,8]{2,1,0:T(1,128)}, f32[1,8]{1,0:T(1,128)}) custom-call(f32[1,8,64,128]{3,2,1,0:T(8,128)S(1)} %get-tuple-element.9.new_ref, f32[4,8,1,128]{3,2,1,0:T(1,128)S(1)} %get-tuple-element.10.parts, f32[4,1,128]{2,1,0:T(1,128)S(1)} %get-tuple-element.11.obs_all), custom_call_target="tpu_custom_call" | custom-call | tf_op jit(solution)/shard_map/finish/pallas_call | solution.py:529

commit v8 on v6

--- a/solution.py
+++ b/solution.py
@@ -139,7 +139,6 @@
     for load in loads[4:]:
         load.start()
 
-
     def exchange(src, dst_at, peers, axis, me, send_sem, recv_sem):
         copies = []
         for d in range(1, peers):
@@ -223,59 +222,6 @@
         load.wait()
     set_flow(0, 0, frac(sat[0], mob[0]))
     set_flow(0, last, frac(sat[last], mob[last]))
-    pl.semaphore_wait(barrier, tiles * members - 1)
-    send(0, 6)
-
-    loads[10].wait()
-    obs_line[...] = jnp.zeros_like(obs_line)
-    obs_line[0:SUBSTEPS, 0:wells_dev] = obs_ref[...]
-    lines = [jnp.zeros((1, LANES), jnp.float32)] * parts.shape[2]
-    for k in range(SUBSTEPS):
-        row, lane = divmod(k * wells, LANES)
-        lines[row] = lines[row] + pltpu.roll(
-            obs_line[k : k + 1, :], lane + tile * wells_dev, 1
-        )
-    packed = jnp.concatenate(lines, axis=0)
-    obs_all[tile] = jnp.where(packed == 0.0, 1.0, packed)
-    obs_copies = exchange(obs_all.at[tile], obs_all.at[tile], tiles, "tile", tile, obs_send, obs_recv)
-
-    def first_flow(i, carry):
-        set_flow(0, i, frac(sat[i], mob[i]))
-        return carry
-
-    for load in loads[4:6]:
-        load.wait()
-    lax.fori_loop(1, last, first_flow, 0)
-    for load in loads[6:10]:
-        load.wait()
-
-    col_ids = lax.broadcasted_iota(jnp.int32, (layers, columns), 1)
-    lay_ids = lax.broadcasted_iota(jnp.int32, (layers, columns), 0)
-
-    def spread_of(here, qz_i, qy_i):
-        qz_i = jnp.where(lay_ids > 0, qz_i, 0.0)
-        qy_i = jnp.where(col_ids > 0, qy_i, 0.0)
-        face_z = face(qz_i, pltpu.roll(here, 1, 0), here)
-        face_y = face(qy_i, pltpu.roll(here, 1, 1), here)
-        return (pltpu.roll(face_z, layers - 1, 0) - face_z) + (
-            pltpu.roll(face_y, columns - 1, 1) - face_y
-        )
-
-    def spread(k, i):
-        return spread_of(flow[k, i], qz[i], qy[i])
-
-    def face_at(k, i):
-        return face(qx[i], flow[k, i - 1], flow[k, i])
-
-    def store(k, i, after):
-        if k + 1 < SUBSTEPS:
-            sat[i] = after
-        else:
-            new_ref[0, i] = after
-        value = frac(after, mob[i])
-        set_flow(k + 1, i, value)
-        return value
-
     def set_masks():
         for load in loads[11:]:
             load.wait()
@@ -295,6 +241,60 @@
         )
         well_mask[...] = jnp.where(columns_of(well_ref[...]) == lane_ids, 1.0, 0.0)
 
+    set_masks()
+    pl.semaphore_wait(barrier, tiles * members - 1)
+    send(0, 6)
+
+    loads[10].wait()
+    obs_line[...] = jnp.zeros_like(obs_line)
+    obs_line[0:SUBSTEPS, 0:wells_dev] = obs_ref[...]
+    lines = [jnp.zeros((1, LANES), jnp.float32)] * parts.shape[2]
+    for k in range(SUBSTEPS):
+        row, lane = divmod(k * wells, LANES)
+        lines[row] = lines[row] + pltpu.roll(
+            obs_line[k : k + 1, :], lane + tile * wells_dev, 1
+        )
+    packed = jnp.concatenate(lines, axis=0)
+    obs_all[tile] = jnp.where(packed == 0.0, 1.0, packed)
+    obs_copies = exchange(obs_all.at[tile], obs_all.at[tile], tiles, "tile", tile, obs_send, obs_recv)
+
+    def first_flow(i, carry):
+        set_flow(0, i, frac(sat[i], mob[i]))
+        return carry
+
+    for load in loads[4:6]:
+        load.wait()
+    lax.fori_loop(1, last, first_flow, 0)
+    for load in loads[6:10]:
+        load.wait()
+
+    col_ids = lax.broadcasted_iota(jnp.int32, (layers, columns), 1)
+    lay_ids = lax.broadcasted_iota(jnp.int32, (layers, columns), 0)
+
+    def spread_of(here, qz_i, qy_i):
+        qz_i = jnp.where(lay_ids > 0, qz_i, 0.0)
+        qy_i = jnp.where(col_ids > 0, qy_i, 0.0)
+        face_z = face(qz_i, pltpu.roll(here, 1, 0), here)
+        face_y = face(qy_i, pltpu.roll(here, 1, 1), here)
+        return (pltpu.roll(face_z, layers - 1, 0) - face_z) + (
+            pltpu.roll(face_y, columns - 1, 1) - face_y
+        )
+
+    def spread(k, i):
+        return spread_of(flow[k, i], qz[i], qy[i])
+
+    def face_at(k, i):
+        return face(qx[i], flow[k, i - 1], flow[k, i])
+
+    def store(k, i, after):
+        if k + 1 < SUBSTEPS:
+            sat[i] = after
+        else:
+            new_ref[0, i] = after
+        value = frac(after, mob[i])
+        set_flow(k + 1, i, value)
+        return value
+
     step_rates = []
     two = 2 * layers
     four = 4 * layers
@@ -325,7 +325,6 @@
     partial[0] = sat[0] - pore[0] * (face_lo + spread(0, 0))
     partial[1] = sat[last] - pore[last] * (spread(0, last) - face_hi)
     qx_first = jnp.where(has_lo, qx[0], 0.0)
-    set_masks()
     found_first = gather(0, two, cells)
     receive(0, 2)
 

time: 18.5 us -> 19.3 us (1.043)
  Pallas kernels: 17.7 us -> 18.5 us
    pallas_call x1, Pallas kernels: 17 us -> 17.8 us  [body(): pl.pallas_call(functools.partial(kernel, tiles, members), out_shape=(pltp...]
where the time goes in v8:
time: 19.3 us; the launch traced here: 19.2 us
  Pallas kernels  18.5 us (96%)
  between operations  0.64 us (3%)
    pallas_call x1, Pallas kernels, body(): pl.pallas_call(functools.partial(kernel, tiles, members), out_shape=(pltp...  17.8 us
    pallas_call x1, Pallas kernels, body(): pl.pallas_call(finish, out_shape=(jax.ShapeDtypeStruct(sat.shape, f32), j...  0.75 us

profile of v8, /device:TPU:0, one launch (start us, length us, event | category | flops | bytes accessed | tf_op | source)
XLA Modules:
  0.0 19.2 jit_solution(13267917271499707265)
XLA Ops:
  0.6 17.8 %transport.1 = (f32[1,8,64,128]{3,2,1,0:T(8,128)S(1)}, f32[4,8,1,128]{3,2,1,0:T(1,128)S(1)}, f32[4,1,128]{2,1,0:T(1,128)S(1)}) custom-call(f32[1,8,64,128]{3,2,1,0:T(8,128)} %sat_hbm.1, f32[1,8,64,128]{3,2,1,0:T(8,128)} %mob_hbm.1, f32[1,8,64,128]{3,2,1,0:T(8,128)} %pore_hbm.1, f32[1,8,64,128]{3,2,1,0:T(8,128)} %qx_hbm.1, f32[1,8,64,128]{3,2,1,0:T(8,128)} %qy_hbm.1, ...), custom_call_target="tpu_custom_call" | custom-call | flops 19660800 | bytes 1835008 | tf_op jit(solution)/shard_map/transport/pallas_call | solution.py:481
  18.4 0.7 %finish.1 = (f32[1,8,64,128]{3,2,1,0:T(8,128)}, f32[3,1,8]{2,1,0:T(1,128)}, f32[1,8]{1,0:T(1,128)}) custom-call(f32[1,8,64,128]{3,2,1,0:T(8,128)S(1)} %get-tuple-element.9.new_ref, f32[4,8,1,128]{3,2,1,0:T(1,128)S(1)} %get-tuple-element.10.parts, f32[4,1,128]{2,1,0:T(1,128)S(1)} %get-tuple-element.11.obs_all), custom_call_target="tpu_custom_call" | custom-call | tf_op jit(solution)/shard_map/finish/pallas_call | solution.py:528
